TPU v7x, 32 devices: a whole 2x2x4 slice. The times are simulated.
32 devices in a mesh: tm: 2 (over x), space: 16 (over z, y, core).
Axes of the slice: x: 2, y: 2, z: 4, core: 2. Of those that a mesh axis runs over, the one named last changes fastest.
Arguments:
- initial_states: float32 [2, 5, 16, 96, 128], P('tm', None, 'space'), may hold values from -6 to 6
- terminal_states: float32 [2, 5, 16, 96, 128], P('tm', None, 'space'), may hold values from -6 to 6
- forcing: float32 [2, 2, 5, 16, 96, 128], P(None, None, None, 'space'), may hold values from -6 to 6
- density_mean: float32 [16, 96, 128], P('space'), may hold values from 0.5 to 2
- velocity_mean: float32 [3, 16, 96, 128], P(None, 'space'), may hold values from -1 to 1
- pressure_mean: float32 [16, 96, 128], P('space'), may hold values from 0.5 to 2
- sponge: float32 [16, 96, 128], P('space'), may hold values from 0.05 to 1
Outputs:
- next_initial: float32 [2, 5, 16, 96, 128], P('tm', None, 'space')
- next_terminal: float32 [2, 5, 16, 96, 128], P('tm', None, 'space')
- response: float32 [2, 2, 5, 16, 96, 128], P(None, None, None, 'space')
- adjoint_projection: float32 [2, 2, 5, 16, 96, 128], P(None, None, None, 'space', 'tm')
All inputs are finite; a program needn't handle non-finite values.
Results may differ from a plain program's by a relative error of at most 0.00002.
Values sent between devices are 32-bit elements; how exact they have to be, the bound alone decides.
A program may use at most 64 MiB of HBM per device.

v0:
```python
import math

import jax
import jax.numpy as jnp
from jax import lax
from jax.sharding import PartitionSpec as P

STEPS = 1
NFREQ = 2


viscosity = 0.05
time_step = 0.25


def with_halo(block, sides, width):
    for axis, dim in sides:
        count = lax.axis_size(axis)
        forward = [(i, i + 1) for i in range(count - 1)]
        backward = [(target, source) for source, target in forward]
        low = lax.ppermute(
            lax.slice_in_dim(block, block.shape[dim] - width, None, axis=dim), axis, forward
        )
        high = lax.ppermute(lax.slice_in_dim(block, 0, width, axis=dim), axis, backward)
        block = jnp.concatenate([low, block, high], axis=dim)
    return block


def passed_along(value, axis, steps):
    count = lax.axis_size(axis)
    pairs = [(source, (source + steps) % count) for source in range(count)]
    return lax.ppermute(value, axis, pairs)


def shifted_pair(field, axis_number):
    widths = [(0, 0)] * field.ndim
    widths[axis_number] = (1, 1)
    padded = jnp.pad(field, widths)
    length = field.shape[axis_number]
    return (
        lax.slice_in_dim(padded, 2, length + 2, axis=axis_number),
        lax.slice_in_dim(padded, 0, length, axis=axis_number),
    )


def forward_rhs(state_padded, density, velocity, pressure, sponge):
    state = state_padded[:, 1:-1]
    grad_x = 0.5 * (state_padded[:, 2:] - state_padded[:, :-2])
    y_plus, y_minus = shifted_pair(state, 2)
    z_plus, z_minus = shifted_pair(state, 3)
    grad_y = 0.5 * (y_plus - y_minus)
    grad_z = 0.5 * (z_plus - z_minus)
    laplace = (
        state_padded[:, 2:]
        + state_padded[:, :-2]
        + y_plus
        + y_minus
        + z_plus
        + z_minus
        - 6.0 * state
    )
    advect = velocity[0] * grad_x + velocity[1] * grad_y + velocity[2] * grad_z
    diverge = grad_x[1] + grad_y[2] + grad_z[3]
    inverse = 1.0 / density
    rows = [
        -advect[0] - density * diverge,
        -advect[1] - inverse * grad_x[4] + viscosity * laplace[1],
        -advect[2] - inverse * grad_y[4] + viscosity * laplace[2],
        -advect[3] - inverse * grad_z[4] + viscosity * laplace[3],
        -advect[4] - pressure * diverge + viscosity * laplace[4],
    ]
    return jnp.stack(rows) - sponge * state


def flux_rows(adjoint, density, inverse, speed, pressure, direction):
    rows = [speed * adjoint[index] for index in range(5)]
    rows[1 + direction] = rows[1 + direction] + density * adjoint[0] + pressure * adjoint[4]
    rows[4] = rows[4] + adjoint[1 + direction] * inverse
    return jnp.stack(rows)


def wave_factors(half_count, total_steps):
    cosines = []
    sines = []
    for freq_index in range(NFREQ):
        turns = (freq_index + 1) * half_count % (2 * total_steps)
        angle = 2.0 * math.pi / (2 * total_steps) * jnp.asarray(turns).astype(jnp.float32)
        cosines.append(jnp.cos(angle))
        sines.append(jnp.sin(angle))
    return (cosines, sines)


def forcing_value(coeffs, half_count, total_steps):
    cosines, sines = wave_factors(half_count, total_steps)
    value = jnp.zeros(coeffs.shape[2:], jnp.float32)
    for freq_index in range(NFREQ):
        value = (
            value
            + coeffs[freq_index, 0] * cosines[freq_index]
            - coeffs[freq_index, 1] * sines[freq_index]
        )
    return value


def sample_terms(state, half_count, total_steps):
    cosines, sines = wave_factors(half_count, total_steps)
    return jnp.stack([jnp.stack([state * cosines[k], -state * sines[k]]) for k in range(NFREQ)])


def rk_step(state, half_count, sign_value, operator, coeffs, total_steps):
    first = operator(state) + forcing_value(coeffs, half_count, total_steps)
    second = operator(state + 0.5 * time_step * first) + forcing_value(
        coeffs, half_count + sign_value, total_steps
    )
    third = operator(state + 0.5 * time_step * second) + forcing_value(
        coeffs, half_count + sign_value, total_steps
    )
    fourth = operator(state + time_step * third) + forcing_value(
        coeffs, half_count + 2 * sign_value, total_steps
    )
    return state + time_step / 6.0 * (first + 2.0 * second + 2.0 * third + fourth)


def per_device(
    initial_states, terminal_states, forcing, density_mean, velocity_mean, pressure_mean, sponge
):
    slab_index = lax.axis_index("tm")
    total_steps = lax.axis_size("tm") * STEPS
    inverse = 1.0 / density_mean
    visc_mask = jnp.array([0.0, 1.0, 1.0, 1.0, 1.0], jnp.float32).reshape(5, 1, 1, 1) * viscosity

    def operate(state):
        padded = with_halo(state, (("space", 1),), 1)
        return forward_rhs(padded, density_mean, velocity_mean, pressure_mean, sponge)

    state = initial_states[0]
    step_index = 0
    half_count = 2 * (slab_index * STEPS + step_index)
    response = sample_terms(state, half_count, total_steps)
    state = rk_step(state, half_count, 1, operate, forcing, total_steps)
    next_initial = passed_along(state[None], "tm", 1)
    response = lax.psum(response, "tm") / total_steps
    reaction = 2.0 * response
    coeff_padded = with_halo(
        jnp.stack([density_mean, inverse, velocity_mean[0], pressure_mean]), (("space", 1),), 1
    )

    def along_x(adjoint):
        adj_padded = with_halo(adjoint, (("space", 1),), 1)
        flux = flux_rows(
            adj_padded, coeff_padded[0], coeff_padded[1], coeff_padded[2], coeff_padded[3], 0
        )
        return 0.5 * (flux[:, 2:] - flux[:, :-2]) + visc_mask * (
            adj_padded[:, 2:] + adj_padded[:, :-2] - 2.0 * adjoint
        )

    def adjoint_operate(adjoint):
        result = along_x(adjoint) - sponge * adjoint
        for direction in (1, 2):
            flux = flux_rows(
                adjoint, density_mean, inverse, velocity_mean[direction], pressure_mean, direction
            )
            flux_plus, flux_minus = shifted_pair(flux, 1 + direction)
            near_plus, near_minus = shifted_pair(adjoint, 1 + direction)
            result = (
                result
                + 0.5 * (flux_plus - flux_minus)
                + visc_mask * (near_plus + near_minus - 2.0 * adjoint)
            )
        return result

    adjoint = terminal_states[0]
    step_index = 0
    half_count = 2 * (slab_index * STEPS + STEPS - step_index)
    adjoint = rk_step(adjoint, half_count, -1, adjoint_operate, reaction, total_steps)
    projection = sample_terms(adjoint, half_count - 2, total_steps)
    next_terminal = passed_along(adjoint[None], "tm", -1)
    projection = lax.psum_scatter(projection, "tm", scatter_dimension=4, tiled=True) / total_steps
    return (next_initial, next_terminal, response, projection)


def solution(mesh):
    return jax.shard_map(
        per_device,
        mesh=mesh,
        in_specs=(
            P("tm", None, "space", None, None),
            P("tm", None, "space", None, None),
            P(None, None, None, "space", None, None),
            P("space", None, None),
            P(None, "space", None, None),
            P("space", None, None),
            P("space", None, None),
        ),
        out_specs=(
            P("tm", None, "space", None, None),
            P("tm", None, "space", None, None),
            P(None, None, None, "space", None, None),
            P(None, None, None, "space", "tm", None),
        ),
        check_vma=False,
    )
```

profile of v0, /device:TPU:17, one launch (start us, length us, event | category | flops | bytes accessed | tf_op | source)
XLA Modules:
  0.0 168.4 jit_solution(393295546387270556)
XLA Ops:
  7.2 0.9 constant_dynamic-update-slice_fusion.49
  8.1 0.9 constant_dynamic-update-slice_fusion.44
  10.3 2.6 %collective-permute-start.10 = (f32[4,1,96,128]{3,2,1,0:T(8,128)}, f32[4,1,96,128]{3,2,1,0:T(8,128)}, u32[]{:S(2)}, u32[]{:S(2)}) collective-permute-start(f32[4,1,96,128]{3,2,1,0:T(8,128)} %pad_maximum_fusion.7), channel_id=1, source_target_pairs={{1,0},{2,1},{3,2},{4,3},{5,4},{6,5},{7,6},{8,7},{9,8},{10,9},{11,1... | collective-permute-start | bytes 589832 | tf_op jit(solution)/shard_map/ppermute | solution.py:24
  12.9 3.0 %collective-permute-start.9 = (f32[4,1,96,128]{3,2,1,0:T(8,128)}, f32[4,1,96,128]{3,2,1,0:T(8,128)}, u32[]{:S(2)}, u32[]{:S(2)}) collective-permute-start(f32[4,1,96,128]{3,2,1,0:T(8,128)} %pad_maximum_fusion.7), channel_id=1, source_target_pairs={{0,1},{1,2},{2,3},{3,4},{4,5},{5,6},{6,7},{7,8},{8,9},{9,10},{10,1... | collective-permute-start | bytes 589832 | tf_op jit(solution)/shard_map/ppermute | solution.py:21
  15.9 2.4 %collective-permute-start.11 = (f32[5,1,96,128]{3,2,1,0:T(8,128)S(1)}, f32[5,1,96,128]{3,2,1,0:T(8,128)S(1)}, u32[]{:S(2)}, u32[]{:S(2)}) collective-permute-start(f32[5,1,96,128]{3,2,1,0:T(8,128)S(1)} %bitcast.1033), channel_id=1, source_target_pairs={{0,1},{1,2},{2,3},{3,4},{4,5},{5,6},{6,7},{7,8},{8,9},{9,10},{10,1... | collective-permute-start | bytes 737288 | tf_op jit(solution)/shard_map/ppermute | solution.py:21
  18.4 1.9 %collective-permute-start.12 = (f32[5,1,96,128]{3,2,1,0:T(8,128)S(1)}, f32[5,1,96,128]{3,2,1,0:T(8,128)}, u32[]{:S(2)}, u32[]{:S(2)}) collective-permute-start(f32[5,1,96,128]{3,2,1,0:T(8,128)S(1)} %bitcast.1034), channel_id=1, source_target_pairs={{1,0},{2,1},{3,2},{4,3},{5,4},{6,5},{7,6},{8,7},{9,8},{10,9},{11,1... | collective-permute-start | bytes 737288 | tf_op jit(solution)/shard_map/ppermute | solution.py:24
  20.8 1.0 pad_maximum_fusion
  21.9 3.8 %collective-permute-start = (f32[5,1,96,128]{3,2,1,0:T(8,128)S(1)}, f32[5,1,96,128]{3,2,1,0:T(8,128)}, u32[]{:S(2)}, u32[]{:S(2)}) collective-permute-start(f32[5,1,96,128]{3,2,1,0:T(8,128)S(1)} %bitcast.1040), channel_id=1, source_target_pairs={{1,0},{2,1},{3,2},{4,3},{5,4},{6,5},{7,6},{8,7},{9,8},{10,9},{11,1... | collective-permute-start | bytes 737288 | tf_op jit(solution)/shard_map/ppermute | solution.py:24
  26.5 2.0 %collective-permute-start.1 = (f32[5,1,96,128]{3,2,1,0:T(8,128)S(1)}, f32[5,1,96,128]{3,2,1,0:T(8,128)}, u32[]{:S(2)}, u32[]{:S(2)}) collective-permute-start(f32[5,1,96,128]{3,2,1,0:T(8,128)S(1)} %bitcast.1041), channel_id=1, source_target_pairs={{0,1},{1,2},{2,3},{3,4},{4,5},{5,6},{6,7},{7,8},{8,9},{9,10},{10,1... | collective-permute-start | bytes 737288 | tf_op jit(solution)/shard_map/ppermute | solution.py:21
  28.6 1.1 pad_maximum_fusion.6
  29.7 1.0 pad_maximum_fusion.2
  34.1 28.2 %all-reduce.26.cloned.1.call-done = f32[2,2,5,1,96,128]{5,4,2,3,1,0:T(8,128)} async-done(((f32[2,2,5,1,96,128]{5,4,2,3,1,0:T(8,128)}), f32[2,2,5,1,96,128]{5,4,2,3,1,0:T(8,128)}) %all-reduce.26.cloned.1.call-update) | async-done | bytes 983056 | tf_op jit(solution)/shard_map/psum | solution.py:142
  63.0 2.6 %multiply_add_fusion = (f32[5,1,96,128]{3,2,1,0:T(8,128)S(1)}, f32[5,1,96,128]{3,2,1,0:T(8,128)}) fusion(f32[1,5,1,96,128]{4,3,2,1,0:T(8,128)S(1)} %copy-done.2, f32[]{:T(128)S(6)} %sin.51, f32[2,2,5,1,96,128]{5,4,2,3,1,0:T(8,128)} %all-reduce.26.cloned.1.call-done, f32[]{:T(128)S(6)} %cos.51, f32[]{:T(128)S(6)} %sin.50, f32[]{:T(128)S(6)} %cos.50, ...), kind=kLoop, calls=%fused_computation.199 | loop fusion | flops 2027520 | bytes 3489828 | tf_op jit(solution)/shard_map/add | solution.py:112
  65.6 3.7 %collective-permute-start.13 = (f32[5,1,96,128]{3,2,1,0:T(8,128)S(1)}, f32[5,1,96,128]{3,2,1,0:T(8,128)S(1)}, u32[]{:S(2)}, u32[]{:S(2)}) collective-permute-start(f32[5,1,96,128]{3,2,1,0:T(8,128)S(1)} %get-tuple-element.15), channel_id=1, source_target_pairs={{0,1},{1,2},{2,3},{3,4},{4,5},{5,6},{6,7},{7,8},{8,9},{9,10},{10,1... | collective-permute-start | bytes 737288 | tf_op jit(solution)/shard_map/ppermute | solution.py:21
  69.3 1.9 %collective-permute-start.14 = (f32[5,1,96,128]{3,2,1,0:T(8,128)S(1)}, f32[5,1,96,128]{3,2,1,0:T(8,128)S(1)}, u32[]{:S(2)}, u32[]{:S(2)}) collective-permute-start(f32[5,1,96,128]{3,2,1,0:T(8,128)S(1)} %get-tuple-element.15), channel_id=1, source_target_pairs={{1,0},{2,1},{3,2},{4,3},{5,4},{6,5},{7,6},{8,7},{9,8},{10,9},{11,1... | collective-permute-start | bytes 737288 | tf_op jit(solution)/shard_map/ppermute | solution.py:24
  71.3 1.1 collective-permute-done.13
  72.4 4.4 %collective-permute-done.14 = f32[5,1,96,128]{3,2,1,0:T(8,128)S(1)} collective-permute-done((f32[5,1,96,128]{3,2,1,0:T(8,128)S(1)}, f32[5,1,96,128]{3,2,1,0:T(8,128)S(1)}, u32[]{:S(2)}, u32[]{:S(2)}) %collective-permute-start.14) | collective-permute-done | bytes 245792 | tf_op jit(solution)/shard_map/ppermute | solution.py:24
  77.0 1.1 copy-done.3
  78.1 1.1 bitcast_add_fusion.2
  79.2 1.9 %collective-permute-start.15 = (f32[5,1,96,128]{3,2,0,1:T(8,128)S(1)}, f32[5,1,96,128]{3,2,0,1:T(8,128)S(1)}, u32[]{:S(2)}, u32[]{:S(2)}) collective-permute-start(f32[5,1,96,128]{3,2,0,1:T(8,128)S(1)} %get-tuple-element.12), channel_id=1, source_target_pairs={{0,1},{1,2},{2,3},{3,4},{4,5},{5,6},{6,7},{7,8},{8,9},{9,10},{10,1... | collective-permute-start | bytes 737288 | tf_op jit(solution)/shard_map/ppermute | solution.py:21
  81.1 2.4 %collective-permute-start.16 = (f32[5,1,96,128]{3,2,0,1:T(8,128)S(1)}, f32[5,1,96,128]{3,2,0,1:T(8,128)S(1)}, u32[]{:S(2)}, u32[]{:S(2)}) collective-permute-start(f32[5,1,96,128]{3,2,0,1:T(8,128)S(1)} %get-tuple-element.12), channel_id=1, source_target_pairs={{1,0},{2,1},{3,2},{4,3},{5,4},{6,5},{7,6},{8,7},{9,8},{10,9},{11,1... | collective-permute-start | bytes 737288 | tf_op jit(solution)/shard_map/ppermute | solution.py:24
  84.3 5.1 %collective-permute-done.16 = f32[5,1,96,128]{3,2,0,1:T(8,128)S(1)} collective-permute-done((f32[5,1,96,128]{3,2,0,1:T(8,128)S(1)}, f32[5,1,96,128]{3,2,0,1:T(8,128)S(1)}, u32[]{:S(2)}, u32[]{:S(2)}) %collective-permute-start.16) | collective-permute-done | bytes 245792 | tf_op jit(solution)/shard_map/ppermute | solution.py:24
  89.6 0.7 copy-done.8
  90.4 1.1 fusion.82
  91.7 1.7 multiply_subtract_fusion.8
  94.7 0.8 fusion.47
  95.5 1.9 %collective-permute-start.2 = (f32[5,1,96,128]{3,2,1,0:T(8,128)}, f32[5,1,96,128]{3,2,1,0:T(8,128)}, u32[]{:S(2)}, u32[]{:S(2)}) collective-permute-start(f32[5,1,96,128]{3,2,1,0:T(8,128)} %fusion.47), channel_id=1, source_target_pairs={{1,0},{2,1},{3,2},{4,3},{5,4},{6,5},{7,6},{8,7},{9,8},{10,9},{11,1... | collective-permute-start | bytes 737288 | tf_op jit(solution)/shard_map/ppermute | solution.py:24
  97.4 3.6 %collective-permute-start.3 = (f32[5,1,96,128]{3,2,1,0:T(8,128)}, f32[5,1,96,128]{3,2,1,0:T(8,128)}, u32[]{:S(2)}, u32[]{:S(2)}) collective-permute-start(f32[5,1,96,128]{3,2,1,0:T(8,128)} %fusion.47), channel_id=1, source_target_pairs={{0,1},{1,2},{2,3},{3,4},{4,5},{5,6},{6,7},{7,8},{8,9},{9,10},{10,1... | collective-permute-start | bytes 737288 | tf_op jit(solution)/shard_map/ppermute | solution.py:21
  102.1 2.8 %collective-permute-start.17 = (f32[5,1,96,128]{3,2,0,1:T(8,128)S(1)}, f32[5,1,96,128]{3,2,0,1:T(8,128)S(1)}, u32[]{:S(2)}, u32[]{:S(2)}) collective-permute-start(f32[5,1,96,128]{3,2,0,1:T(8,128)S(1)} %get-tuple-element.10), channel_id=1, source_target_pairs={{0,1},{1,2},{2,3},{3,4},{4,5},{5,6},{6,7},{7,8},{8,9},{9,10},{10,1... | collective-permute-start | bytes 737288 | tf_op jit(solution)/shard_map/ppermute | solution.py:21
  104.9 1.9 %collective-permute-start.18 = (f32[5,1,96,128]{3,2,0,1:T(8,128)S(1)}, f32[5,1,96,128]{3,2,0,1:T(8,128)S(1)}, u32[]{:S(2)}, u32[]{:S(2)}) collective-permute-start(f32[5,1,96,128]{3,2,0,1:T(8,128)S(1)} %get-tuple-element.10), channel_id=1, source_target_pairs={{1,0},{2,1},{3,2},{4,3},{5,4},{6,5},{7,6},{8,7},{9,8},{10,9},{11,1... | collective-permute-start | bytes 737288 | tf_op jit(solution)/shard_map/ppermute | solution.py:24
  107.1 3.4 %multiply_subtract_fusion.6 = (f32[5,1,96,128]{3,2,1,0:T(8,128)S(1)}, f32[5,1,96,128]{3,2,1,0:T(8,128)S(1)}, f32[5,1,96,128]{3,2,1,0:T(8,128)S(1)}, f32[5,1,96,128]{3,2,1,0:T(8,128)S(1)}, f32[5,1,96,128]{3,2,1,0:T(8,128)S(1)}) fusion(f32[5,1,96,128]{3,2,1,0:T(8,128)} %fusion.47, f32[5,1,96,128]{3,2,1,0:T(8,128)} %collective-permute-done.2, ...), kind=kLoop, calls=%fused_computation.205 | loop fusion | flops 1228800 | bytes 2113536 | tf_op jit(solution)/shard_map/sub | solution.py:54
  110.7 0.8 copy-done.9
  111.6 1.1 fusion.51
  112.7 4.3 %collective-permute-start.4 = (f32[5,1,96,128]{3,2,1,0:T(8,128)S(1)}, f32[5,1,96,128]{3,2,1,0:T(8,128)S(1)}, u32[]{:S(2)}, u32[]{:S(2)}) collective-permute-start(f32[5,1,96,128]{3,2,1,0:T(8,128)S(1)} %get-tuple-element.47), channel_id=1, source_target_pairs={{1,0},{2,1},{3,2},{4,3},{5,4},{6,5},{7,6},{8,7},{9,8},{10,9},{11,1... | collective-permute-start | bytes 737288 | tf_op jit(solution)/shard_map/ppermute | solution.py:24
  116.9 2.0 %collective-permute-start.5 = (f32[5,1,96,128]{3,2,1,0:T(8,128)S(1)}, f32[5,1,96,128]{3,2,1,0:T(8,128)S(1)}, u32[]{:S(2)}, u32[]{:S(2)}) collective-permute-start(f32[5,1,96,128]{3,2,1,0:T(8,128)S(1)} %get-tuple-element.47), channel_id=1, source_target_pairs={{0,1},{1,2},{2,3},{3,4},{4,5},{5,6},{6,7},{7,8},{8,9},{9,10},{10,1... | collective-permute-start | bytes 737288 | tf_op jit(solution)/shard_map/ppermute | solution.py:21
  119.3 0.8 copy-done.33
  121.2 3.1 %collective-permute-done.5 = f32[5,1,96,128]{3,2,1,0:T(8,128)S(1)} collective-permute-done((f32[5,1,96,128]{3,2,1,0:T(8,128)S(1)}, f32[5,1,96,128]{3,2,1,0:T(8,128)S(1)}, u32[]{:S(2)}, u32[]{:S(2)}) %collective-permute-start.5) | collective-permute-done | bytes 245792 | tf_op jit(solution)/shard_map/ppermute | solution.py:21
  125.7 3.5 %collective-permute-start.6 = (f32[5,1,96,128]{3,2,1,0:T(8,128)S(1)}, f32[5,1,96,128]{3,2,1,0:T(8,128)}, u32[]{:S(2)}, u32[]{:S(2)}) collective-permute-start(f32[5,1,96,128]{3,2,1,0:T(8,128)S(1)} %fusion.55), channel_id=1, source_target_pairs={{1,0},{2,1},{3,2},{4,3},{5,4},{6,5},{7,6},{8,7},{9,8},{10,9},{11,1... | collective-permute-start | bytes 737288 | tf_op jit(solution)/shard_map/ppermute | solution.py:24
  129.1 2.8 %collective-permute-start.7 = (f32[5,1,96,128]{3,2,1,0:T(8,128)S(1)}, f32[5,1,96,128]{3,2,1,0:T(8,128)}, u32[]{:S(2)}, u32[]{:S(2)}) collective-permute-start(f32[5,1,96,128]{3,2,1,0:T(8,128)S(1)} %fusion.55), channel_id=1, source_target_pairs={{0,1},{1,2},{2,3},{3,4},{4,5},{5,6},{6,7},{7,8},{8,9},{9,10},{10,1... | collective-permute-start | bytes 737288 | tf_op jit(solution)/shard_map/ppermute | solution.py:21
  132.0 1.0 pad_maximum_fusion.1
  134.0 2.0 %collective-permute-done.7 = f32[5,1,96,128]{3,2,1,0:T(8,128)} collective-permute-done((f32[5,1,96,128]{3,2,1,0:T(8,128)S(1)}, f32[5,1,96,128]{3,2,1,0:T(8,128)}, u32[]{:S(2)}, u32[]{:S(2)}) %collective-permute-start.7) | collective-permute-done | bytes 245792 | tf_op jit(solution)/shard_map/ppermute | solution.py:21
  136.0 1.5 multiply_subtract_fusion.3
  137.7 0.8 copy-done.39
  139.5 1.0 multiply_bitcast_fusion
  140.6 1.4 collective-permute-done.19
  142.6 9.5 %collective-permute-done.8 = f32[1,5,1,96,128]{4,3,2,1,0:T(8,128)S(1)} collective-permute-done((f32[1,5,1,96,128]{4,3,2,1,0:T(8,128)S(1)}, f32[1,5,1,96,128]{4,3,2,1,0:T(8,128)S(1)}, u32[]{:S(2)}, u32[]{:S(2)}) %collective-permute-start.8) | collective-permute-done | bytes 245792 | tf_op jit(solution)/shard_map/ppermute | solution.py:32
  152.1 5.9 %reduce-scatter.2.cloned.1.call-done = f32[2,2,5,1,48,128]{5,4,3,2,1,0:T(8,128)} async-done(((f32[2,2,5,1,96,128]{5,4,3,2,1,0:T(8,128)}), f32[2,2,5,1,48,128]{5,4,3,2,1,0:T(8,128)}) %reduce-scatter.2.cloned.1.call-update) | async-done | bytes 491536 | tf_op jit(solution)/shard_map/reduce_scatter | solution.py:178
  158.0 1.8 %broadcast_multiply_fusion = f32[2,2,5,1,48,128]{5,4,3,2,1,0:T(8,128)} fusion(f32[2,2,5,1,48,128]{5,4,3,2,1,0:T(8,128)} %reduce-scatter.2.cloned.1.call-done), kind=kLoop, calls=%fused_computation.193 | loop fusion | flops 122880 | bytes 983040 | tf_op jit(solution)/shard_map/div | solution.py:178
  (194 shorter events, 15.9 us)
Async XLA Ops:
  7.2 55.1 %all-reduce.26.cloned.1.call-start = ((), (), s32[]{:S(2)}) async-start(), calls=%async_computation.1 | async-start | bytes 1966080 | tf_op jit(solution)/shard_map/psum | solution.py:142
  8.1 1.5 copy-start.6
  9.0 6.9 %copy-start.2 = (f32[1,5,1,96,128]{4,3,2,1,0:T(8,128)S(1)}, f32[1,5,1,96,128]{4,3,2,1,0:T(8,128)}, u32[]{:S(2)}) copy-start(f32[1,5,1,96,128]{4,3,2,1,0:T(8,128)} %param.9) | copy-start | bytes 737284
  9.0 1.3 copy-start.24
  9.0 11.6 %copy-start.5 = (f32[1,5,1,96,128]{4,3,2,1,0:T(8,128)S(1)}, f32[1,5,1,96,128]{4,3,2,1,0:T(8,128)}, u32[]{:S(2)}) copy-start(f32[1,5,1,96,128]{4,3,2,1,0:T(8,128)} %param.8) | copy-start | bytes 737284
  10.3 16.2 %collective-permute-start.10 = (f32[4,1,96,128]{3,2,1,0:T(8,128)}, f32[4,1,96,128]{3,2,1,0:T(8,128)}, u32[]{:S(2)}, u32[]{:S(2)}) collective-permute-start(f32[4,1,96,128]{3,2,1,0:T(8,128)} %pad_maximum_fusion.7), channel_id=1, source_target_pairs={{1,0},{2,1},{3,2},{4,3},{5,4},{6,5},{7,6},{8,7},{9,8},{10,9},{11,1... | collective-permute-start | bytes 589832 | tf_op jit(solution)/shard_map/ppermute | solution.py:24
  12.9 15.7 %collective-permute-start.9 = (f32[4,1,96,128]{3,2,1,0:T(8,128)}, f32[4,1,96,128]{3,2,1,0:T(8,128)}, u32[]{:S(2)}, u32[]{:S(2)}) collective-permute-start(f32[4,1,96,128]{3,2,1,0:T(8,128)} %pad_maximum_fusion.7), channel_id=1, source_target_pairs={{0,1},{1,2},{2,3},{3,4},{4,5},{5,6},{6,7},{7,8},{8,9},{9,10},{10,1... | collective-permute-start | bytes 589832 | tf_op jit(solution)/shard_map/ppermute | solution.py:21
  15.9 13.7 %collective-permute-start.11 = (f32[5,1,96,128]{3,2,1,0:T(8,128)S(1)}, f32[5,1,96,128]{3,2,1,0:T(8,128)S(1)}, u32[]{:S(2)}, u32[]{:S(2)}) collective-permute-start(f32[5,1,96,128]{3,2,1,0:T(8,128)S(1)} %bitcast.1033), channel_id=1, source_target_pairs={{0,1},{1,2},{2,3},{3,4},{4,5},{5,6},{6,7},{7,8},{8,9},{9,10},{10,1... | collective-permute-start | bytes 737288 | tf_op jit(solution)/shard_map/ppermute | solution.py:21
  18.4 11.3 %collective-permute-start.12 = (f32[5,1,96,128]{3,2,1,0:T(8,128)S(1)}, f32[5,1,96,128]{3,2,1,0:T(8,128)}, u32[]{:S(2)}, u32[]{:S(2)}) collective-permute-start(f32[5,1,96,128]{3,2,1,0:T(8,128)S(1)} %bitcast.1034), channel_id=1, source_target_pairs={{1,0},{2,1},{3,2},{4,3},{5,4},{6,5},{7,6},{8,7},{9,8},{10,9},{11,1... | collective-permute-start | bytes 737288 | tf_op jit(solution)/shard_map/ppermute | solution.py:24
  21.9 136.1 %reduce-scatter.2.cloned.1.call-start = ((), (), s32[]{:S(2)}) async-start(), calls=%async_computation.2 | async-start | bytes 1474560 | tf_op jit(solution)/shard_map/reduce_scatter | solution.py:178
  21.9 69.7 %collective-permute-start = (f32[5,1,96,128]{3,2,1,0:T(8,128)S(1)}, f32[5,1,96,128]{3,2,1,0:T(8,128)}, u32[]{:S(2)}, u32[]{:S(2)}) collective-permute-start(f32[5,1,96,128]{3,2,1,0:T(8,128)S(1)} %bitcast.1040), channel_id=1, source_target_pairs={{1,0},{2,1},{3,2},{4,3},{5,4},{6,5},{7,6},{8,7},{9,8},{10,9},{11,1... | collective-permute-start | bytes 737288 | tf_op jit(solution)/shard_map/ppermute | solution.py:24
  26.4 2.2 %copy-start.23 = (f32[1,1,96,128]{3,2,1,0:T(8,128)S(1)}, f32[1,1,96,128]{3,2,1,0:T(8,128)}, u32[]{:S(2)}) copy-start(f32[1,1,96,128]{3,2,1,0:T(8,128)} %copy-done.22) | copy-start | bytes 147460
  26.4 2.2 %copy-start.25 = (f32[1,1,96,128]{3,2,1,0:T(8,128)S(1)}, f32[1,1,96,128]{3,2,1,0:T(8,128)}, u32[]{:S(2)}) copy-start(f32[1,1,96,128]{3,2,1,0:T(8,128)} %copy-done.24) | copy-start | bytes 147460
  26.5 2.1 %copy-start.26 = (f32[5,1,96,128]{3,2,1,0:T(8,128)}, f32[5,1,96,128]{3,2,1,0:T(8,128)S(1)}, u32[]{:S(2)}) copy-start(f32[5,1,96,128]{3,2,1,0:T(8,128)S(1)} %get-tuple-element.75) | copy-start | bytes 737284
  26.5 2.1 %copy-start.30 = (f32[5,1,96,128]{3,2,1,0:T(8,128)}, f32[5,1,96,128]{3,2,1,0:T(8,128)S(1)}, u32[]{:S(2)}) copy-start(f32[5,1,96,128]{3,2,1,0:T(8,128)S(1)} %get-tuple-element.76) | copy-start | bytes 737284
  26.5 65.2 %collective-permute-start.1 = (f32[5,1,96,128]{3,2,1,0:T(8,128)S(1)}, f32[5,1,96,128]{3,2,1,0:T(8,128)}, u32[]{:S(2)}, u32[]{:S(2)}) collective-permute-start(f32[5,1,96,128]{3,2,1,0:T(8,128)S(1)} %bitcast.1041), channel_id=1, source_target_pairs={{0,1},{1,2},{2,3},{3,4},{4,5},{5,6},{6,7},{7,8},{8,9},{9,10},{10,1... | collective-permute-start | bytes 737288 | tf_op jit(solution)/shard_map/ppermute | solution.py:21
  33.5 28.9 %copy-start.7 = (f32[1,96,128]{2,1,0:T(8,128)S(1)}, f32[1,96,128]{2,1,0:T(8,128)}, u32[]{:S(2)}) copy-start(f32[1,96,128]{2,1,0:T(8,128)} %param.14) | copy-start | bytes 147460
  33.5 28.9 %copy-start.27 = (f32[5,1,96,128]{3,2,1,0:T(8,128)S(1)}, f32[5,1,96,128]{3,2,1,0:T(8,128)}, u32[]{:S(2)}) copy-start(f32[5,1,96,128]{3,2,1,0:T(8,128)} %copy-done.26) | copy-start | bytes 737284
  33.5 28.9 %copy-start.31 = (f32[5,1,96,128]{3,2,1,0:T(8,128)S(1)}, f32[5,1,96,128]{3,2,1,0:T(8,128)}, u32[]{:S(2)}) copy-start(f32[5,1,96,128]{3,2,1,0:T(8,128)} %copy-done.30) | copy-start | bytes 737284
  65.6 6.8 %collective-permute-start.13 = (f32[5,1,96,128]{3,2,1,0:T(8,128)S(1)}, f32[5,1,96,128]{3,2,1,0:T(8,128)S(1)}, u32[]{:S(2)}, u32[]{:S(2)}) collective-permute-start(f32[5,1,96,128]{3,2,1,0:T(8,128)S(1)} %get-tuple-element.15), channel_id=1, source_target_pairs={{0,1},{1,2},{2,3},{3,4},{4,5},{5,6},{6,7},{7,8},{8,9},{9,10},{10,1... | collective-permute-start | bytes 737288 | tf_op jit(solution)/shard_map/ppermute | solution.py:21
  69.3 7.5 %collective-permute-start.14 = (f32[5,1,96,128]{3,2,1,0:T(8,128)S(1)}, f32[5,1,96,128]{3,2,1,0:T(8,128)S(1)}, u32[]{:S(2)}, u32[]{:S(2)}) collective-permute-start(f32[5,1,96,128]{3,2,1,0:T(8,128)S(1)} %get-tuple-element.15), channel_id=1, source_target_pairs={{1,0},{2,1},{3,2},{4,3},{5,4},{6,5},{7,6},{8,7},{9,8},{10,9},{11,1... | collective-permute-start | bytes 737288 | tf_op jit(solution)/shard_map/ppermute | solution.py:24
  79.2 5.0 %collective-permute-start.15 = (f32[5,1,96,128]{3,2,0,1:T(8,128)S(1)}, f32[5,1,96,128]{3,2,0,1:T(8,128)S(1)}, u32[]{:S(2)}, u32[]{:S(2)}) collective-permute-start(f32[5,1,96,128]{3,2,0,1:T(8,128)S(1)} %get-tuple-element.12), channel_id=1, source_target_pairs={{0,1},{1,2},{2,3},{3,4},{4,5},{5,6},{6,7},{7,8},{8,9},{9,10},{10,1... | collective-permute-start | bytes 737288 | tf_op jit(solution)/shard_map/ppermute | solution.py:21
  81.1 8.3 %collective-permute-start.16 = (f32[5,1,96,128]{3,2,0,1:T(8,128)S(1)}, f32[5,1,96,128]{3,2,0,1:T(8,128)S(1)}, u32[]{:S(2)}, u32[]{:S(2)}) collective-permute-start(f32[5,1,96,128]{3,2,0,1:T(8,128)S(1)} %get-tuple-element.12), channel_id=1, source_target_pairs={{1,0},{2,1},{3,2},{4,3},{5,4},{6,5},{7,6},{8,7},{9,8},{10,9},{11,1... | collective-permute-start | bytes 737288 | tf_op jit(solution)/shard_map/ppermute | solution.py:24
  91.6 1.8 %copy-start.12 = (f32[96,128]{1,0:T(8,128)}, f32[96,128]{1,0:T(8,128)S(1)}, u32[]{:S(2)}) copy-start(f32[96,128]{1,0:T(8,128)S(1)} %get-tuple-element.106) | copy-start | bytes 147460
  91.6 1.8 %copy-start.14 = (f32[96,128]{1,0:T(8,128)}, f32[96,128]{1,0:T(8,128)S(1)}, u32[]{:S(2)}) copy-start(f32[96,128]{1,0:T(8,128)S(1)} %get-tuple-element.107) | copy-start | bytes 147460
  91.6 1.8 %copy-start.16 = (f32[96,128]{1,0:T(8,128)}, f32[96,128]{1,0:T(8,128)S(1)}, u32[]{:S(2)}) copy-start(f32[96,128]{1,0:T(8,128)S(1)} %get-tuple-element.108) | copy-start | bytes 147460
  91.6 1.8 %copy-start.28 = (f32[5,1,96,128]{3,2,1,0:T(8,128)}, f32[5,1,96,128]{3,2,1,0:T(8,128)S(1)}, u32[]{:S(2)}) copy-start(f32[5,1,96,128]{3,2,1,0:T(8,128)S(1)} %get-tuple-element.69) | copy-start | bytes 737284
  91.6 1.8 %copy-start.32 = (f32[5,1,96,128]{3,2,1,0:T(8,128)}, f32[5,1,96,128]{3,2,1,0:T(8,128)S(1)}, u32[]{:S(2)}) copy-start(f32[5,1,96,128]{3,2,1,0:T(8,128)S(1)} %get-tuple-element.70) | copy-start | bytes 737284
  93.4 1.3 copy-start.4
  95.5 11.3 %collective-permute-start.2 = (f32[5,1,96,128]{3,2,1,0:T(8,128)}, f32[5,1,96,128]{3,2,1,0:T(8,128)}, u32[]{:S(2)}, u32[]{:S(2)}) collective-permute-start(f32[5,1,96,128]{3,2,1,0:T(8,128)} %fusion.47), channel_id=1, source_target_pairs={{1,0},{2,1},{3,2},{4,3},{5,4},{6,5},{7,6},{8,7},{9,8},{10,9},{11,1... | collective-permute-start | bytes 737288 | tf_op jit(solution)/shard_map/ppermute | solution.py:24
  97.4 9.7 %collective-permute-start.3 = (f32[5,1,96,128]{3,2,1,0:T(8,128)}, f32[5,1,96,128]{3,2,1,0:T(8,128)}, u32[]{:S(2)}, u32[]{:S(2)}) collective-permute-start(f32[5,1,96,128]{3,2,1,0:T(8,128)} %fusion.47), channel_id=1, source_target_pairs={{0,1},{1,2},{2,3},{3,4},{4,5},{5,6},{6,7},{7,8},{8,9},{9,10},{10,1... | collective-permute-start | bytes 737288 | tf_op jit(solution)/shard_map/ppermute | solution.py:21
  101.2 5.9 %copy-start.17 = (f32[96,128]{1,0:T(8,128)S(1)}, f32[96,128]{1,0:T(8,128)}, u32[]{:S(2)}) copy-start(f32[96,128]{1,0:T(8,128)} %copy-done.16) | copy-start | bytes 147460
  101.4 5.7 %copy-start.15 = (f32[96,128]{1,0:T(8,128)S(1)}, f32[96,128]{1,0:T(8,128)}, u32[]{:S(2)}) copy-start(f32[96,128]{1,0:T(8,128)} %copy-done.14) | copy-start | bytes 147460
  101.4 5.7 %copy-start.13 = (f32[96,128]{1,0:T(8,128)S(1)}, f32[96,128]{1,0:T(8,128)}, u32[]{:S(2)}) copy-start(f32[96,128]{1,0:T(8,128)} %copy-done.12) | copy-start | bytes 147460
  102.1 16.9 %collective-permute-start.17 = (f32[5,1,96,128]{3,2,0,1:T(8,128)S(1)}, f32[5,1,96,128]{3,2,0,1:T(8,128)S(1)}, u32[]{:S(2)}, u32[]{:S(2)}) collective-permute-start(f32[5,1,96,128]{3,2,0,1:T(8,128)S(1)} %get-tuple-element.10), channel_id=1, source_target_pairs={{0,1},{1,2},{2,3},{3,4},{4,5},{5,6},{6,7},{7,8},{8,9},{9,10},{10,1... | collective-permute-start | bytes 737288 | tf_op jit(solution)/shard_map/ppermute | solution.py:21
  104.9 14.1 %collective-permute-start.18 = (f32[5,1,96,128]{3,2,0,1:T(8,128)S(1)}, f32[5,1,96,128]{3,2,0,1:T(8,128)S(1)}, u32[]{:S(2)}, u32[]{:S(2)}) collective-permute-start(f32[5,1,96,128]{3,2,0,1:T(8,128)S(1)} %get-tuple-element.10), channel_id=1, source_target_pairs={{1,0},{2,1},{3,2},{4,3},{5,4},{6,5},{7,6},{8,7},{9,8},{10,9},{11,1... | collective-permute-start | bytes 737288 | tf_op jit(solution)/shard_map/ppermute | solution.py:24
  110.7 2.0 %copy-start.36 = (f32[1,5,1,96,128]{4,3,2,1,0:T(8,128)}, f32[1,5,1,96,128]{4,3,2,1,0:T(8,128)S(1)}, u32[]{:S(2)}) copy-start(f32[1,5,1,96,128]{4,3,2,1,0:T(8,128)S(1)} %get-tuple-element.27) | copy-start | bytes 737284
  112.6 12.9 %copy-start.10 = (f32[1,1,5,1,96,128]{5,4,2,3,1,0:T(8,128)}, f32[1,1,5,1,96,128]{5,4,2,3,1,0:T(8,128)S(1)}, u32[]{:S(2)}) copy-start(f32[1,1,5,1,96,128]{5,4,2,3,1,0:T(8,128)S(1)} %get-tuple-element.48) | copy-start | bytes 737284
  112.7 8.5 %collective-permute-start.4 = (f32[5,1,96,128]{3,2,1,0:T(8,128)S(1)}, f32[5,1,96,128]{3,2,1,0:T(8,128)S(1)}, u32[]{:S(2)}, u32[]{:S(2)}) collective-permute-start(f32[5,1,96,128]{3,2,1,0:T(8,128)S(1)} %get-tuple-element.47), channel_id=1, source_target_pairs={{1,0},{2,1},{3,2},{4,3},{5,4},{6,5},{7,6},{8,7},{9,8},{10,9},{11,1... | collective-permute-start | bytes 737288 | tf_op jit(solution)/shard_map/ppermute | solution.py:24
  116.9 7.4 %collective-permute-start.5 = (f32[5,1,96,128]{3,2,1,0:T(8,128)S(1)}, f32[5,1,96,128]{3,2,1,0:T(8,128)S(1)}, u32[]{:S(2)}, u32[]{:S(2)}) collective-permute-start(f32[5,1,96,128]{3,2,1,0:T(8,128)S(1)} %get-tuple-element.47), channel_id=1, source_target_pairs={{0,1},{1,2},{2,3},{3,4},{4,5},{5,6},{6,7},{7,8},{8,9},{9,10},{10,1... | collective-permute-start | bytes 737288 | tf_op jit(solution)/shard_map/ppermute | solution.py:21
  119.3 1.3 copy-start.21
  121.1 3.2 %copy-start.18 = (f32[96,128]{1,0:T(8,128)S(1)}, f32[96,128]{1,0:T(8,128)}, u32[]{:S(2)}) copy-start(f32[96,128]{1,0:T(8,128)} %copy-done.16) | copy-start | bytes 147460
  125.7 8.4 %collective-permute-start.6 = (f32[5,1,96,128]{3,2,1,0:T(8,128)S(1)}, f32[5,1,96,128]{3,2,1,0:T(8,128)}, u32[]{:S(2)}, u32[]{:S(2)}) collective-permute-start(f32[5,1,96,128]{3,2,1,0:T(8,128)S(1)} %fusion.55), channel_id=1, source_target_pairs={{1,0},{2,1},{3,2},{4,3},{5,4},{6,5},{7,6},{8,7},{9,8},{10,9},{11,1... | collective-permute-start | bytes 737288 | tf_op jit(solution)/shard_map/ppermute | solution.py:24
  129.1 6.9 %collective-permute-start.7 = (f32[5,1,96,128]{3,2,1,0:T(8,128)S(1)}, f32[5,1,96,128]{3,2,1,0:T(8,128)}, u32[]{:S(2)}, u32[]{:S(2)}) collective-permute-start(f32[5,1,96,128]{3,2,1,0:T(8,128)S(1)} %fusion.55), channel_id=1, source_target_pairs={{0,1},{1,2},{2,3},{3,4},{4,5},{5,6},{6,7},{7,8},{8,9},{9,10},{10,1... | collective-permute-start | bytes 737288 | tf_op jit(solution)/shard_map/ppermute | solution.py:21
  133.1 8.9 %collective-permute-start.19 = (f32[1,5,1,96,128]{4,3,1,2,0:T(8,128)S(1)}, f32[1,5,1,96,128]{4,3,1,2,0:T(8,128)S(1)}, u32[]{:S(2)}, u32[]{:S(2)}) collective-permute-start(f32[1,5,1,96,128]{4,3,1,2,0:T(8,128)S(1)} %bitcast.1065), channel_id=1, source_target_pairs={{0,16},{16,0},{1,17},{17,1},{2,18},{18,2},{3,19},{19,3},{4,20},{20... | collective-permute-start | bytes 737288 | tf_op jit(solution)/shard_map/ppermute | solution.py:32
  137.6 1.3 copy-start.11
  137.6 1.4 copy-start.35
  139.4 12.7 %collective-permute-start.8 = (f32[1,5,1,96,128]{4,3,2,1,0:T(8,128)S(1)}, f32[1,5,1,96,128]{4,3,2,1,0:T(8,128)S(1)}, u32[]{:S(2)}, u32[]{:S(2)}) collective-permute-start(f32[1,5,1,96,128]{4,3,2,1,0:T(8,128)S(1)} %fusion.81), channel_id=1, source_target_pairs={{0,16},{16,0},{1,17},{17,1},{2,18},{18,2},{3,19},{19,3},{4,20},{20... | collective-permute-start | bytes 737288 | tf_op jit(solution)/shard_map/ppermute | solution.py:32
  (17 other events, 15.5 us)
Sparse Core Ops, SparseCore 0:
  22.0 40.2 all-reduce.25
  133.2 24.7 reduce-scatter.1
where the time goes:
time: 170 us; the launch traced here: 168 us
  waiting for transfers between devices  62 us (36%)
  starting transfers between devices  49.1 us (29%)
  other arithmetic  29.2 us (17%)
  between operations  17.2 us (10%)
  local copies, waits for them, and re-layouts  10.8 us (6%)
    psum x1, waiting for transfers between devices, per_device(): response = lax.psum(response, 'tm') / total_steps  28.2 us
    ppermute x9, starting transfers between devices, with_halo(): lax.ppermute(lax.slice_in_dim(block, block.shape[dim] - width, None, axis...  24.4 us
    ppermute x9, starting transfers between devices, with_halo(): lax.ppermute(lax.slice_in_dim(block, 0, width, axis=dim), axis, backward)  24.2 us
    ppermute x2, waiting for transfers between devices, passed_along(): return lax.ppermute(value, axis, pairs)  10.8 us
    unnamed x97, local copies, waits for them, and re-layouts  10.8 us
    ppermute x9, waiting for transfers between devices, with_halo(): lax.ppermute(lax.slice_in_dim(block, 0, width, axis=dim), axis, backward)  10.2 us
    sub x4, other arithmetic, forward_rhs(): state_padded[:, 2:] + state_padded[:, :-2] + y_plus + y_minus + z_plus  7.01 us
    ppermute x9, waiting for transfers between devices, with_halo(): lax.ppermute(lax.slice_in_dim(block, block.shape[dim] - width, None, axis...  6.97 us
  transfers between devices with their start and end apart: 22, of which 12 were waited for; matrix products, arithmetic and copies ran while one was open for 13% of the time, Pallas kernels for 0%

commit v1 on v0

v1 whole, which is shorter than its diff:
```python
import functools
import math

import jax
import jax.numpy as jnp
from jax import lax
from jax.experimental import pallas as pl
from jax.experimental.pallas import tpu as pltpu
from jax.sharding import PartitionSpec as P

NFREQ = 2
viscosity = 0.05
time_step = 0.25
MESH = pl.DeviceIdType.MESH

R_INIT, R_COEF, R_TERM, R_F0, R_F1, C_SIB, C_EXT = range(7)
HALO = 7
FINAL = HALO + 24
SLAB = FINAL + 5


def theta(k, half_count, slabs):
    turns = (k + 1) * half_count % (2 * slabs)
    return 2.0 * math.pi * turns / (2 * slabs)


def picked(values, index):
    out = jnp.float32(values[0])
    for j in range(1, len(values)):
        out = jnp.where(index == j, jnp.float32(values[j]), out)
    return out


def force_factors(slab, offset, n):
    rows = []
    for k in range(NFREQ):
        rows.append(picked([math.cos(theta(k, 2 * j + offset, n)) for j in range(n)], slab))
        rows.append(picked([-math.sin(theta(k, 2 * j + offset, n)) for j in range(n)], slab))
    return rows


def react_factor(half_gap, n):
    return 2.0 / n * sum(math.cos(theta(k, half_gap, n)) for k in range(NFREQ))


def shift_y(x, above, below, rows):
    n = x.shape[0]
    minus = jnp.where(rows == 0, above, pltpu.roll(x, 1, 0))
    plus = jnp.where(rows == n - 1, below, pltpu.roll(x, n - 1, 0))
    return plus, minus


def shift_z(x, lanes):
    n = x.shape[1]
    minus = jnp.where(lanes == 0, 0.0, pltpu.roll(x, 1, 1))
    plus = jnp.where(lanes == n - 1, 0.0, pltpu.roll(x, n - 1, 1))
    return plus, minus


def forward_plane(c, lo, hi, w, halo_row, first, rows, lanes):
    rho, u1, u2, u3, pres, sponge, inv = [w(i) for i in range(7)]
    out = [None] * 5
    for f in range(5):
        v, a, b = c(f), lo(f), hi(f)
        r = halo_row(f)
        yp, ym = shift_y(v, jnp.where(first, 0.0, r), jnp.where(first, r, 0.0), rows)
        zp, zm = shift_z(v, lanes)
        dx, dy, dz = 0.5 * (b - a), 0.5 * (yp - ym), 0.5 * (zp - zm)
        o = -(u1 * dx + u2 * dy + u3 * dz) - sponge * v
        if f > 0:
            o = o + viscosity * ((a + b) + (yp + ym) + (zp + zm) - 6.0 * v)
        if f == 1:
            div = dx
        elif f == 2:
            div = div + dy
        elif f == 3:
            div = div + dz
        elif f == 4:
            out[1] = out[1] - inv * dx
            out[2] = out[2] - inv * dy
            out[3] = out[3] - inv * dz
        out[f] = o
    out[0] = out[0] - rho * div
    out[4] = out[4] - pres * div
    return out


def flux(a, rho, inv, speed, pres, direction):
    rows = [speed * a[i] for i in range(5)]
    rows[1 + direction] = rows[1 + direction] + rho * a[0] + pres * a[4]
    rows[4] = rows[4] + a[1 + direction] * inv
    return rows


def adjoint_plane(c, lo, hi, w, clo, chi, halo_row, first, rows, lanes):
    rho, u1, u2, u3, pres, sponge, inv = [w(i) for i in range(7)]
    a = [c(f) for f in range(5)]
    al, ah = [lo(f) for f in range(5)], [hi(f) for f in range(5)]
    fl = flux(al, clo(0), clo(3), clo(1), clo(2), 0)
    fh = flux(ah, chi(0), chi(3), chi(1), chi(2), 0)
    fy = flux(a, rho, inv, u2, pres, 1)
    fz = flux(a, rho, inv, u3, pres, 2)
    out = []
    for f in range(5):
        r = halo_row(8 + f)
        yp, ym = shift_y(fy[f], jnp.where(first, 0.0, r), jnp.where(first, r, 0.0), rows)
        zp, zm = shift_z(fz[f], lanes)
        o = 0.5 * ((fh[f] - fl[f]) + (yp - ym) + (zp - zm)) - sponge * a[f]
        if f > 0:
            r = halo_row(f)
            yp, ym = shift_y(a[f], jnp.where(first, 0.0, r), jnp.where(first, r, 0.0), rows)
            zp, zm = shift_z(a[f], lanes)
            o = o + viscosity * ((al[f] + ah[f]) + (yp + ym) + (zp + zm) - 6.0 * a[f])
        out.append(o)
    return out


def kernel(
    n, count, init, term, forcing, dens, vel, pres, spon,
    others, qn, an, ao,
    state, halo, row_out, row_in, coef, coef_halo, coef_send, work_f, f_send, work_init, final,
    send, recv,
):
    tm = lax.axis_index("tm")
    s = lax.axis_index("space")
    group, part, core = s // 4, (s // 2) % 2, s % 2
    other = 1 - part
    half = init.shape[3] // 2
    sibling = s + 1 - 2 * core
    partner = s + 2 - 4 * part
    groups = count // 4
    has_ext = jnp.logical_or(
        jnp.logical_and(core == 0, group > 0), jnp.logical_and(core == 1, group < groups - 1)
    )
    ext = (group + 2 * core - 1) * 4 + part * 2 + 1 - core
    after, before = lax.rem(tm + 1, n), lax.rem(tm + n - 1, n)
    mine = pl.ds(pl.multiple_of(part * half, 8), half)
    theirs = pl.ds(pl.multiple_of(other * half, 8), half)
    first = part == 0

    barrier = pltpu.get_barrier_semaphore()
    greet = [(tm, sibling), (tm, partner), (after, partner)]
    if n > 2:
        greet.append((before, partner))
    greet += [(lax.rem(tm + d, n), s) for d in range(1, n)]
    for who in greet:
        pl.semaphore_signal(barrier, inc=1, device_id=who, device_id_type=MESH)

    @pl.when(has_ext)
    def _():
        pl.semaphore_signal(barrier, inc=1, device_id=(tm, ext), device_id_type=MESH)

    coef_send[0] = dens[0, theirs, :]
    for d in range(3):
        coef_send[1 + d] = vel[d, 0, theirs, :]
    coef_send[4] = pres[0, theirs, :]
    coef_send[5] = spon[0, theirs, :]

    pl.semaphore_wait(barrier, len(greet) + has_ext.astype(jnp.int32))

    def copy(i, src, dst, who):
        return pltpu.make_async_remote_copy(
            src_ref=src, dst_ref=dst, send_sem=send.at[i], recv_sem=recv.at[i],
            device_id=who, device_id_type=MESH,
        )

    started, started_ext = [], []

    def go(i, src, dst, who):
        c = copy(i, src, dst, who)
        c.start()
        started.append(c)
        return c

    def go_ext(i, src, dst):
        c = copy(i, src, dst, (tm, ext))

        @pl.when(has_ext)
        def _():
            c.start()

        started_ext.append(c)
        return c

    def arrived_ext(c):
        @pl.when(has_ext)
        def _():
            c.wait_recv()

    r_init = go(R_INIT, init.at[0, :, 0, theirs, :], state.at[0, 0, part], (tm, partner))
    r_coef = go(R_COEF, coef_send.at[pl.ds(0, 6)], coef.at[part, pl.ds(0, 6)], (tm, partner))
    r_term = go(R_TERM, term.at[0, :, 0, theirs, :], state.at[1, 0, part], (tm, partner))
    slab_copies = [
        go(SLAB + 2 * (d - 1), init.at[0, :, 0], others.at[d - 1], (lax.rem(tm + d, n), s))
        for d in range(1, n)
    ]

    def force(offset, rows):
        factors = force_factors(tm, offset, n)
        return [
            sum(factors[2 * k + r] * forcing[k, r, f, 0, rows, :] for k in range(NFREQ) for r in range(2))
            for f in range(5)
        ]

    for offset in range(2):
        for f, value in enumerate(force(offset, theirs)):
            f_send[offset, f] = value
    r_f0 = go(R_F0, f_send.at[0], work_f.at[0, part], (tm, partner))
    r_f1 = go(R_F1, f_send.at[1], work_f.at[1, part], (tm, partner))

    state[0, 0, part] = init[0, :, 0, mine, :]
    state[1, 0, part] = term[0, :, 0, mine, :]
    coef[part, 0] = dens[0, mine, :]
    for d in range(3):
        coef[part, 1 + d] = vel[d, 0, mine, :]
    coef[part, 4] = pres[0, mine, :]
    coef[part, 5] = spon[0, mine, :]
    for offset in range(2):
        for f, value in enumerate(force(offset, mine)):
            work_f[offset, part, f] = value

    @pl.when(jnp.logical_not(has_ext))
    def _():
        zeros = jnp.zeros(halo.shape[3:], jnp.float32)
        for eq in range(2):
            for stage in range(4):
                halo[eq, stage, 2 * core] = zeros
        coef_halo[2 * core, pl.ds(0, 3)] = jnp.ones((3,) + coef_halo.shape[2:], jnp.float32)

    nrows, nlanes = half, init.shape[4]
    rows = lax.broadcasted_iota(jnp.int32, (nrows, nlanes), 0)
    lanes = lax.broadcasted_iota(jnp.int32, (nrows, nlanes), 1)

    def edge(ref):
        return jnp.where(first, ref[nrows - 1 :, :], ref[0:1, :])

    halos = {}

    def send_halo(eq, stage):
        base = HALO + 3 * (4 * eq + stage)
        y = state.at[eq, stage]
        sib = go(base, y, halo.at[eq, stage, pl.ds(core, 2)], (tm, sibling))
        out = go_ext(base + 1, y.at[core], halo.at[eq, stage, 2 * (1 - core)])
        for k in range(2):
            a = [edge(y.at[k, f]) for f in range(5)]
            for f in range(5):
                row_out[eq, stage, k, f : f + 1, :] = a[f]
            if eq == 1:
                rho, u2, pr, inv = [edge(coef.at[k, i]) for i in (0, 2, 4, 6)]
                for f, value in enumerate(flux(a, rho, inv, u2, pr, 1)):
                    row_out[eq, stage, k, 8 + f : 9 + f, :] = value
        row = go(base + 2, row_out.at[eq, stage], row_in.at[eq, stage], (tm, partner))
        halos[eq, stage] = (sib, out, row)

    def wait_halo(eq, stage):
        sib, out, row = halos[eq, stage]
        sib.wait_recv()
        row.wait_recv()
        arrived_ext(out)

    r_init.wait_recv()
    send_halo(0, 0)
    init_copies = [
        go(
            SLAB + 2 * (d - 1) + 1, state.at[0, 0, other], work_init.at[d - 1, other],
            (lax.rem(tm + d, n), s),
        )
        for d in range(1, n)
    ]
    r_coef.wait_recv()
    for k in range(2):
        for i, source in enumerate((0, 1, 4)):
            coef_send[6 + 3 * k + i] = coef[k, source]
        coef[k, 6] = 1.0 / coef[k, 0]
    c_sib = []
    for k in range(2):
        c_sib.append(
            go(
                SLAB + 2 * (n - 1) + k, coef_send.at[pl.ds(6 + 3 * k, 3)],
                coef_halo.at[core + k, pl.ds(0, 3)], (tm, sibling),
            )
        )
    c_ext = go_ext(
        C_EXT, coef_send.at[pl.ds(6 + 3 * core, 3)], coef_halo.at[2 * (1 - core), pl.ds(0, 3)]
    )
    r_term.wait_recv()
    send_halo(1, 0)

    def react(offset, k, f):
        value = react_factor(offset, n) * state[0, 0, k, f]
        for d in range(1, n):
            value = value + react_factor(offset + 2 * d, n) * work_init[d - 1, k, f]
        return value

    def run_stage(eq, stage):
        wait_halo(eq, stage)
        if stage < 2 and eq == 0:
            (r_f0, r_f1)[stage].wait_recv()
        if eq == 1 and stage == 0:
            for c in c_sib:
                c.wait_recv()
            arrived_ext(c_ext)
            for k in range(3):
                coef_halo[k, 3] = 1.0 / coef_halo[k, 0]
            for d in range(1, n):
                slab_copies[d - 1].wait_recv()
                init_copies[d - 1].wait_recv()
                work_init[d - 1, part] = others[d - 1, :, mine, :]
        step = (0.5 * time_step, 0.5 * time_step, time_step)
        for k in range(2):
            c = lambda f: state[eq, stage, k, f]
            lo = lambda f: halo[eq, stage, k, f]
            hi = lambda f: halo[eq, stage, k + 1, f]
            w = lambda i: coef[k, i]
            row = lambda i: row_in[eq, stage, k, i : i + 1, :]
            if eq == 0:
                out = forward_plane(c, lo, hi, w, row, first, rows, lanes)
            else:
                clo = lambda i: coef_halo[k, i]
                chi = lambda i: coef_halo[k + 1, i]
                out = adjoint_plane(c, lo, hi, w, clo, chi, row, first, rows, lanes)
            for f in range(5):
                if stage < 3:
                    if eq == 0:
                        rate = out[f] + work_f[min(stage, 1), k, f]
                    else:
                        rate = out[f] + react(2 - min(stage, 1), k, f)
                    state[eq, stage + 1, k, f] = state[eq, 0, k, f] + step[stage] * rate
                else:
                    mix = state[eq, 1, k, f] + 2.0 * state[eq, 2, k, f] + state[eq, 3, k, f]
                    final[eq, k, f] = (mix - state[eq, 0, k, f]) * (1.0 / 3.0) + (
                        time_step / 6.0
                    ) * out[f]

    last = []

    def send_final(eq):
        target, place = ((after, qn), (before, an))[eq]
        last.append(go(FINAL + 2 * eq, final.at[eq, other], place.at[:, mine, :], (target, partner)))
        last.append(go(FINAL + 2 * eq + 1, final.at[eq, part], place.at[:, mine, :], (target, s)))
        if eq == 1:
            last.append(go(FINAL + 4, final.at[1, other], ao.at[:, mine, :], (tm, partner)))
            ao[:, mine, :] = final[1, part]

    for stage in range(4):
        for eq in range(2):
            run_stage(eq, stage)
            if stage < 3:
                send_halo(eq, stage + 1)
            else:
                send_final(eq)

    for c in last:
        c.wait_recv()
    for c in started:
        c.wait_send()

    @pl.when(has_ext)
    def _():
        for c in started_ext:
            c.wait_send()


def exchange(n, count, *args):
    ny, nz = args[0].shape[3:]
    half = ny // 2
    f32 = jnp.float32
    plane = jax.ShapeDtypeStruct((5, ny, nz), f32)
    vmem = pl.BlockSpec(memory_space=pltpu.VMEM)
    sems = SLAB + 2 * (n - 1) + 2
    return pl.pallas_call(
        functools.partial(kernel, n, count),
        out_shape=[jax.ShapeDtypeStruct((n - 1, 5, ny, nz), f32), plane, plane, plane],
        in_specs=[vmem] * 7,
        out_specs=[vmem] * 4,
        scratch_shapes=[
            pltpu.VMEM((2, 4, 2, 5, half, nz), f32),
            pltpu.VMEM((2, 4, 3, 5, half, nz), f32),
            pltpu.VMEM((2, 4, 2, 16, nz), f32),
            pltpu.VMEM((2, 4, 2, 16, nz), f32),
            pltpu.VMEM((2, 7, half, nz), f32),
            pltpu.VMEM((3, 4, half, nz), f32),
            pltpu.VMEM((12, half, nz), f32),
            pltpu.VMEM((2, 2, 5, half, nz), f32),
            pltpu.VMEM((2, 5, half, nz), f32),
            pltpu.VMEM((n - 1, 2, 5, half, nz), f32),
            pltpu.VMEM((2, 2, 5, half, nz), f32),
            pltpu.SemaphoreType.DMA((sems,)),
            pltpu.SemaphoreType.DMA((sems,)),
        ],
        compiler_params=pltpu.CompilerParams(
            collective_id=0, has_side_effects=True, vmem_limit_bytes=40 * 1024 * 1024
        ),
    )(*args)


def per_device(n, count, initial, terminal, forcing, density, velocity, pressure, sponge):
    others, qn, an, ao = exchange(
        n, count, initial, terminal, forcing, density, velocity, pressure, sponge
    )
    tm = lax.axis_index("tm")
    states = [initial[0, :, 0]] + [others[d - 1] for d in range(1, n)]

    def factor(function, k, shift):
        return picked([function(theta(k, 2 * ((j + shift) % n), n)) for j in range(n)], tm)

    def amplitudes(fields, shifts):
        rows = []
        for k in range(NFREQ):
            cos = [factor(math.cos, k, shift) / n for shift in shifts]
            sin = [factor(math.sin, k, shift) / n for shift in shifts]
            rows.append(sum(c * v for c, v in zip(cos, fields)))
            rows.append(-sum(c * v for c, v in zip(sin, fields)))
        return jnp.stack(rows).reshape((NFREQ, 2) + fields[0].shape)

    def react(offset):
        return sum(react_factor(offset + 2 * d, n) * states[d] for d in range(n))

    response = amplitudes(states, [-d for d in range(n)])[:, :, :, None]
    factors = force_factors(tm, 0, n)
    force = sum(factors[2 * k + r] * forcing[k, r, :, 0] for k in range(NFREQ) for r in range(2))
    next_initial = qn + (time_step / 6.0) * force
    next_terminal = an + (time_step / 6.0) * react(2)
    adjoint = ao + (time_step / 6.0) * react(0)
    if n == 2:
        rows = initial.shape[3] // n
        own = lax.dynamic_slice_in_dim(adjoint, tm * rows, rows, axis=1)
        far = lax.dynamic_slice_in_dim(next_terminal, tm * rows, rows, axis=1)
        projection = amplitudes([own, far], [0, 1])[:, :, :, None]
    else:
        projection = amplitudes([adjoint], [0])[:, :, :, None]
        projection = lax.psum_scatter(projection, "tm", scatter_dimension=4, tiled=True)
    return (next_initial[None, :, None], next_terminal[None, :, None], response, projection)


def solution(mesh):
    return jax.shard_map(
        functools.partial(per_device, mesh.shape["tm"], mesh.shape["space"]),
        mesh=mesh,
        in_specs=(
            P("tm", None, "space", None, None),
            P("tm", None, "space", None, None),
            P(None, None, None, "space", None, None),
            P("space", None, None),
            P(None, "space", None, None),
            P("space", None, None),
            P("space", None, None),
        ),
        out_specs=(
            P("tm", None, "space", None, None),
            P("tm", None, "space", None, None),
            P(None, None, None, "space", None, None),
            P(None, None, None, "space", "tm", None),
        ),
        check_vma=False,
    )
```

time: 170 us -> 52.8 us (0.31)
  waiting for transfers between devices: 62 us -> 0 us
  starting transfers between devices: 49.1 us -> 0 us
  Pallas kernels: 0 us -> 43.2 us
  other arithmetic: 29.2 us -> 3.9 us
  between operations: 17.2 us -> 0.72 us
  local copies, waits for them, and re-layouts: 10.8 us -> 4.66 us
    ppermute x20 -> x0, starting transfers between devices: 49.1 us -> none  [the longest x9 24.4 us: with_halo(): lax.ppermute(lax.slice_in_dim(block, block.shape[dim] - width, None, axis...]
    pallas_call x0 -> x1, Pallas kernels: none -> 43.2 us  [exchange(): pl.pallas_call(functools.partial(kernel, n, count), out_shape=[jax.ShapeD...]
    psum x1 -> x0, waiting for transfers between devices: 28.2 us -> none  [per_device(): response = lax.psum(response, 'tm') / total_steps]
    ppermute x20 -> x0, waiting for transfers between devices: 28 us -> none  [the longest x2 10.8 us: passed_along(): return lax.ppermute(value, axis, pairs)]
    sub x4 -> x0, other arithmetic: 7.01 us -> none  [forward_rhs(): state_padded[:, 2:] + state_padded[:, :-2] + y_plus + y_minus + z_plus]
    add x7 -> x2, other arithmetic: 7.08 us -> 0.2 us  [the longest x1 0.16 us: amplitudes(): rows.append(sum((c * v for c, v in zip(cos, fields))))]
    unnamed x97 -> x16, local copies, waits for them, and re-layouts: 10.8 us -> 4.66 us
    reduce_scatter x1 -> x0, waiting for transfers between devices: 5.85 us -> none  [per_device(): lax.psum_scatter(projection, 'tm', scatter_dimension=4, tiled=True)]
  transfers between devices with their start and end apart: 22 -> 0, of which waited for: 12 -> 0; matrix products, arithmetic and copies ran while one was open for 13% -> 0% of each run, Pallas kernels for 0% -> 0%
where the time goes in v1:
time: 52.8 us; the launch traced here: 52.5 us
  Pallas kernels  43.2 us (82%)
  local copies, waits for them, and re-layouts  4.66 us (9%)
  other arithmetic  3.9 us (7%)
  between operations  0.72 us (1%)
    pallas_call x1, Pallas kernels, exchange(): pl.pallas_call(functools.partial(kernel, n, count), out_shape=[jax.ShapeD...  43.2 us
    unnamed x16, local copies, waits for them, and re-layouts  4.66 us
    another operation x4, other arithmetic, amplitudes(): return jnp.stack(rows).reshape((NFREQ, 2) + fields[0].shape)  1.91 us

profile of v1, /device:TPU:17, one launch (start us, length us, event | category | flops | bytes accessed | tf_op | source)
XLA Modules:
  0.0 52.5 jit_solution(12763122279139704669)
XLA Ops:
  0.7 0.0 copy-start.1
  0.7 0.0 copy-start.2
  0.7 1.0 %fusion.14 = f32[5,96,128]{2,1,0:T(8,128)S(1)} fusion(f32[1,5,1,96,128]{4,3,2,1,0:T(8,128)} %init.1), kind=kLoop, calls=%fused_computation.27 | loop fusion | flops 61440 | bytes 491520 | tf_op jit(solution)/shard_map/mul | solution.py:417
  1.7 0.0 copy-done.1
  1.7 0.1 copy-done.2
  1.8 0.0 copy-start
  1.8 1.2 %copy-done = f32[2,2,5,1,96,128]{5,4,3,2,1,0:T(8,128)S(1)} copy-done((f32[2,2,5,1,96,128]{5,4,3,2,1,0:T(8,128)S(1)}, f32[2,2,5,1,96,128]{5,4,3,2,1,0:T(8,128)}, u32[]{:S(2)}) %copy-start) | copy-done | bytes 983064
  3.0 0.0 copy-start.3
  3.0 0.9 %copy-done.3 = f32[3,1,96,128]{3,2,1,0:T(8,128)S(1)} copy-done((f32[3,1,96,128]{3,2,1,0:T(8,128)S(1)}, f32[3,1,96,128]{3,2,1,0:T(8,128)}, u32[]{:S(2)}) %copy-start.3) | copy-done | bytes 147480
  3.9 0.0 copy-start.4
  3.9 0.8 %copy-done.4 = f32[1,96,128]{2,1,0:T(8,128)S(1)} copy-done((f32[1,96,128]{2,1,0:T(8,128)S(1)}, f32[1,96,128]{2,1,0:T(8,128)}, u32[]{:S(2)}) %copy-start.4) | copy-done | bytes 49176
  4.7 0.0 copy-start.5
  4.7 0.8 %copy-done.5 = f32[1,96,128]{2,1,0:T(8,128)S(1)} copy-done((f32[1,96,128]{2,1,0:T(8,128)S(1)}, f32[1,96,128]{2,1,0:T(8,128)}, u32[]{:S(2)}) %copy-start.5) | copy-done | bytes 49176
  5.5 0.0 copy-start.6
  5.5 0.8 %copy-done.6 = f32[1,96,128]{2,1,0:T(8,128)S(1)} copy-done((f32[1,96,128]{2,1,0:T(8,128)S(1)}, f32[1,96,128]{2,1,0:T(8,128)}, u32[]{:S(2)}) %copy-start.6) | copy-done | bytes 49176
  6.3 43.2 %shard_map.102 = (f32[1,5,96,128]{3,2,1,0:T(8,128)S(1)}, f32[5,96,128]{2,1,0:T(8,128)S(1)}, f32[5,96,128]{2,1,0:T(8,128)S(1)}, f32[5,96,128]{2,1,0:T(8,128)S(1)}) custom-call(f32[1,5,1,96,128]{4,3,2,1,0:T(8,128)S(1)} %copy-done.1, f32[1,5,1,96,128]{4,3,2,1,0:T(8,128)S(1)} %copy-done.2, f32[2,2,5,1,96,128]{5,4,3,2,1,0:T(8,128)S(1)} %copy-done, ...), custom_call_target="tpu_custom_call" | custom-call | tf_op jit(solution)/shard_map/pallas_call | solution.py:371
  49.5 0.8 %fusion.4 = f32[1,5,1,96,128]{4,3,2,1,0:T(8,128)} fusion(f32[5,96,128]{2,1,0:T(8,128)S(1)} %get-tuple-element.8, f32[2,2,5,1,96,128]{5,4,2,3,1,0:T(8,128)S(1)} %bitcast.64, f32[]{:T(128)S(6)} %select_n.36, f32[]{:T(128)S(6)} %select_n.35), kind=kLoop, calls=%fused_computation.7 | loop fusion | flops 491520 | bytes 1474568
  50.4 0.0 copy-start.7
  50.4 0.2 fusion.6
  50.6 1.0 %pad_maximum_fusion = f32[4,5,96,128]{3,2,1,0:T(8,128)} fusion(f32[1,5,96,128]{3,2,1,0:T(8,128)S(1)} %get-tuple-element.21, f32[1,5,96,128]{3,2,1,0:T(8,128)S(1)} %get-tuple-element.20, f32[1,5,96,128]{3,2,1,0:T(8,128)S(1)} %get-tuple-element.19, f32[1,5,96,128]{3,2,1,0:T(8,128)S(1)} %get-tuple-element.18), kind=kLoop, calls=%fused_computation | loop fusion | flops 737280 | bytes 1966080 | tf_op jit(solution)/shard_map/stack | solution.py:414
  51.6 0.0 copy-done.7
  51.6 0.8 %pad_maximum_fusion.1 = f32[4,5,48,128]{3,2,1,0:T(8,128)} fusion(f32[1,5,48,128]{3,2,1,0:T(8,128)S(1)} %get-tuple-element.23, f32[1,5,48,128]{3,2,1,0:T(8,128)S(1)} %get-tuple-element.24, f32[1,5,48,128]{3,2,1,0:T(8,128)S(1)} %get-tuple-element.22, f32[1,5,48,128]{3,2,1,0:T(8,128)S(1)} %get-tuple-element.16), kind=kLoop, calls=%fused_computation.1 | loop fusion | flops 368640 | bytes 983040 | tf_op jit(solution)/shard_map/stack | solution.py:414
  (3 shorter events, 0.1 us)
Async XLA Ops:
  0.7 1.1 %copy-start.1 = (f32[1,5,1,96,128]{4,3,2,1,0:T(8,128)S(1)}, f32[1,5,1,96,128]{4,3,2,1,0:T(8,128)}, u32[]{:S(2)}) copy-start(f32[1,5,1,96,128]{4,3,2,1,0:T(8,128)} %init.1) | copy-start | bytes 737284
  0.7 1.2 %copy-start.2 = (f32[1,5,1,96,128]{4,3,2,1,0:T(8,128)S(1)}, f32[1,5,1,96,128]{4,3,2,1,0:T(8,128)}, u32[]{:S(2)}) copy-start(f32[1,5,1,96,128]{4,3,2,1,0:T(8,128)} %term.1) | copy-start | bytes 737284
  1.8 1.2 %copy-start = (f32[2,2,5,1,96,128]{5,4,3,2,1,0:T(8,128)S(1)}, f32[2,2,5,1,96,128]{5,4,3,2,1,0:T(8,128)}, u32[]{:S(2)}) copy-start(f32[2,2,5,1,96,128]{5,4,3,2,1,0:T(8,128)} %forcing.1) | copy-start | bytes 2949124
  3.0 0.9 %copy-start.3 = (f32[3,1,96,128]{3,2,1,0:T(8,128)S(1)}, f32[3,1,96,128]{3,2,1,0:T(8,128)}, u32[]{:S(2)}) copy-start(f32[3,1,96,128]{3,2,1,0:T(8,128)} %vel.1) | copy-start | bytes 442372
  3.9 0.8 %copy-start.4 = (f32[1,96,128]{2,1,0:T(8,128)S(1)}, f32[1,96,128]{2,1,0:T(8,128)}, u32[]{:S(2)}) copy-start(f32[1,96,128]{2,1,0:T(8,128)} %dens.1) | copy-start | bytes 147460
  4.7 0.8 %copy-start.5 = (f32[1,96,128]{2,1,0:T(8,128)S(1)}, f32[1,96,128]{2,1,0:T(8,128)}, u32[]{:S(2)}) copy-start(f32[1,96,128]{2,1,0:T(8,128)} %pres.1) | copy-start | bytes 147460
  5.5 0.8 %copy-start.6 = (f32[1,96,128]{2,1,0:T(8,128)S(1)}, f32[1,96,128]{2,1,0:T(8,128)}, u32[]{:S(2)}) copy-start(f32[1,96,128]{2,1,0:T(8,128)} %spon.1) | copy-start | bytes 147460
  50.4 1.2 %copy-start.7 = (f32[5,96,128]{2,1,0:T(8,128)}, f32[5,96,128]{2,1,0:T(8,128)S(1)}, u32[]{:S(2)}) copy-start(f32[5,96,128]{2,1,0:T(8,128)S(1)} %fusion.13) | copy-start | bytes 737284

commit v2 on v1

--- a/solution.py
+++ b/solution.py
@@ -12,12 +12,6 @@
 viscosity = 0.05
 time_step = 0.25
 MESH = pl.DeviceIdType.MESH
-
-R_INIT, R_COEF, R_TERM, R_F0, R_F1, C_SIB, C_EXT = range(7)
-HALO = 7
-FINAL = HALO + 24
-SLAB = FINAL + 5
-
 
 def theta(k, half_count, slabs):
     turns = (k + 1) * half_count % (2 * slabs)
@@ -116,10 +110,10 @@
 
 
 def kernel(
-    n, count, init, term, forcing, dens, vel, pres, spon,
+    n, count, sems, init, term, forcing_hbm, dens, vel, pres, spon,
     others, qn, an, ao,
     state, halo, row_out, row_in, coef, coef_halo, coef_send, work_f, f_send, work_init, final,
-    send, recv,
+    forcing, send, recv, local,
 ):
     tm = lax.axis_index("tm")
     s = lax.axis_index("space")
@@ -139,9 +133,9 @@
     first = part == 0
 
     barrier = pltpu.get_barrier_semaphore()
-    greet = [(tm, sibling), (tm, partner), (after, partner)]
-    if n > 2:
-        greet.append((before, partner))
+    greet = [(tm, sibling), (tm, partner), (before, partner), (after, partner)]
+    if n == 2:
+        greet.pop()
     greet += [(lax.rem(tm + d, n), s) for d in range(1, n)]
     for who in greet:
         pl.semaphore_signal(barrier, inc=1, device_id=who, device_id_type=MESH)
@@ -150,30 +144,41 @@
     def _():
         pl.semaphore_signal(barrier, inc=1, device_id=(tm, ext), device_id_type=MESH)
 
-    coef_send[0] = dens[0, theirs, :]
-    for d in range(3):
-        coef_send[1 + d] = vel[d, 0, theirs, :]
-    coef_send[4] = pres[0, theirs, :]
-    coef_send[5] = spon[0, theirs, :]
+    fetches = []
+
+    def fetch(src, dst):
+        c = pltpu.make_async_copy(src, dst, local.at[len(fetches)])
+        c.start()
+        fetches.append(c)
+
+    fetch(forcing_hbm, forcing)
+    fetch(dens.at[:, mine, :], coef.at[part, pl.ds(0, 1)])
+    fetch(vel.at[:, 0, mine, :], coef.at[part, pl.ds(1, 3)])
+    fetch(pres.at[:, mine, :], coef.at[part, pl.ds(4, 1)])
+    fetch(spon.at[:, mine, :], coef.at[part, pl.ds(5, 1)])
+    fetch(init.at[0, :, 0, mine, :], work_init.at[n - 2, part])
 
     pl.semaphore_wait(barrier, len(greet) + has_ext.astype(jnp.int32))
 
-    def copy(i, src, dst, who):
+    started, started_ext = [], []
+
+    def make(src, dst, who, out=None, into=None):
+        if out is None:
+            out = into = len(started) + len(started_ext)
+            assert out < sems - 2
         return pltpu.make_async_remote_copy(
-            src_ref=src, dst_ref=dst, send_sem=send.at[i], recv_sem=recv.at[i],
+            src_ref=src, dst_ref=dst, send_sem=send.at[out], recv_sem=recv.at[into],
             device_id=who, device_id_type=MESH,
         )
 
-    started, started_ext = [], []
-
-    def go(i, src, dst, who):
-        c = copy(i, src, dst, who)
+    def go(src, dst, who):
+        c = make(src, dst, who)
         c.start()
         started.append(c)
         return c
 
-    def go_ext(i, src, dst):
-        c = copy(i, src, dst, (tm, ext))
+    def go_ext(src, dst):
+        c = make(src, dst, (tm, ext))
 
         @pl.when(has_ext)
         def _():
@@ -187,34 +192,39 @@
         def _():
             c.wait_recv()
 
-    r_init = go(R_INIT, init.at[0, :, 0, theirs, :], state.at[0, 0, part], (tm, partner))
-    r_coef = go(R_COEF, coef_send.at[pl.ds(0, 6)], coef.at[part, pl.ds(0, 6)], (tm, partner))
-    r_term = go(R_TERM, term.at[0, :, 0, theirs, :], state.at[1, 0, part], (tm, partner))
+    s_theirs = go(init.at[0, :, 0, theirs, :], others.at[0, :, theirs, :], (after, s))
+    r_coef = [
+        go(dens.at[:, theirs, :], coef.at[part, pl.ds(0, 1)], (tm, partner)),
+        go(vel.at[:, 0, theirs, :], coef.at[part, pl.ds(1, 3)], (tm, partner)),
+        go(pres.at[:, theirs, :], coef.at[part, pl.ds(4, 1)], (tm, partner)),
+        go(spon.at[:, theirs, :], coef.at[part, pl.ds(5, 1)], (tm, partner)),
+    ]
+    s_mine = go(init.at[0, :, 0, mine, :], others.at[0, :, mine, :], (after, s))
+    r_term = [
+        go(term.at[0, :, 0, theirs, :], state.at[1, 0, part], (before, partner)),
+        go(term.at[0, :, 0, mine, :], state.at[1, 0, part], (before, s)),
+    ]
     slab_copies = [
-        go(SLAB + 2 * (d - 1), init.at[0, :, 0], others.at[d - 1], (lax.rem(tm + d, n), s))
-        for d in range(1, n)
+        go(init.at[0, :, 0], others.at[d - 1], (lax.rem(tm + d, n), s)) for d in range(2, n)
     ]
 
     def force(offset, rows):
-        factors = force_factors(tm, offset, n)
+        factors = force_factors(before, offset, n)
         return [
             sum(factors[2 * k + r] * forcing[k, r, f, 0, rows, :] for k in range(NFREQ) for r in range(2))
             for f in range(5)
         ]
 
-    for offset in range(2):
-        for f, value in enumerate(force(offset, theirs)):
-            f_send[offset, f] = value
-    r_f0 = go(R_F0, f_send.at[0], work_f.at[0, part], (tm, partner))
-    r_f1 = go(R_F1, f_send.at[1], work_f.at[1, part], (tm, partner))
-
-    state[0, 0, part] = init[0, :, 0, mine, :]
-    state[1, 0, part] = term[0, :, 0, mine, :]
-    coef[part, 0] = dens[0, mine, :]
-    for d in range(3):
-        coef[part, 1 + d] = vel[d, 0, mine, :]
-    coef[part, 4] = pres[0, mine, :]
-    coef[part, 5] = spon[0, mine, :]
+    fetches[0].wait()
+    for f, value in enumerate(force(0, theirs)):
+        f_send[0, f] = value
+    r_f0 = go(f_send.at[0], work_f.at[0, part], (tm, partner))
+    for f, value in enumerate(force(1, theirs)):
+        f_send[1, f] = value
+    s_theirs.wait_recv()
+    r_init = go(others.at[0, :, theirs, :], state.at[0, 0, part], (tm, partner))
+    r_f1 = go(f_send.at[1], work_f.at[1, part], (tm, partner))
+
     for offset in range(2):
         for f, value in enumerate(force(offset, mine)):
             work_f[offset, part, f] = value
@@ -237,10 +247,9 @@
     halos = {}
 
     def send_halo(eq, stage):
-        base = HALO + 3 * (4 * eq + stage)
         y = state.at[eq, stage]
-        sib = go(base, y, halo.at[eq, stage, pl.ds(core, 2)], (tm, sibling))
-        out = go_ext(base + 1, y.at[core], halo.at[eq, stage, 2 * (1 - core)])
+        sib = go(y, halo.at[eq, stage, pl.ds(core, 2)], (tm, sibling))
+        out = go_ext(y.at[core], halo.at[eq, stage, 2 * (1 - core)])
         for k in range(2):
             a = [edge(y.at[k, f]) for f in range(5)]
             for f in range(5):
@@ -249,7 +258,7 @@
                 rho, u2, pr, inv = [edge(coef.at[k, i]) for i in (0, 2, 4, 6)]
                 for f, value in enumerate(flux(a, rho, inv, u2, pr, 1)):
                     row_out[eq, stage, k, 8 + f : 9 + f, :] = value
-        row = go(base + 2, row_out.at[eq, stage], row_in.at[eq, stage], (tm, partner))
+        row = go(row_out.at[eq, stage], row_in.at[eq, stage], (tm, partner))
         halos[eq, stage] = (sib, out, row)
 
     def wait_halo(eq, stage):
@@ -258,38 +267,35 @@
         row.wait_recv()
         arrived_ext(out)
 
+    for c in fetches[1:]:
+        c.wait()
+    for c in r_coef:
+        c.wait_recv()
+    for k in range(2):
+        for i, source in enumerate((0, 1, 4)):
+            coef_send[3 * k + i] = coef[k, source]
+        coef[k, 6] = 1.0 / coef[k, 0]
+    c_sib = [
+        go(coef_send.at[pl.ds(3 * k, 3)], coef_halo.at[core + k, pl.ds(0, 3)], (tm, sibling))
+        for k in range(2)
+    ]
+    c_ext = go_ext(coef_send.at[pl.ds(3 * core, 3)], coef_halo.at[2 * (1 - core), pl.ds(0, 3)])
+    s_mine.wait_recv()
+    state[0, 0, part] = others[0, :, mine, :]
     r_init.wait_recv()
     send_halo(0, 0)
     init_copies = [
-        go(
-            SLAB + 2 * (d - 1) + 1, state.at[0, 0, other], work_init.at[d - 1, other],
-            (lax.rem(tm + d, n), s),
-        )
+        go(state.at[0, 0, other], work_init.at[d - 1, other], (lax.rem(tm + d, n), s))
         for d in range(1, n)
     ]
-    r_coef.wait_recv()
-    for k in range(2):
-        for i, source in enumerate((0, 1, 4)):
-            coef_send[6 + 3 * k + i] = coef[k, source]
-        coef[k, 6] = 1.0 / coef[k, 0]
-    c_sib = []
-    for k in range(2):
-        c_sib.append(
-            go(
-                SLAB + 2 * (n - 1) + k, coef_send.at[pl.ds(6 + 3 * k, 3)],
-                coef_halo.at[core + k, pl.ds(0, 3)], (tm, sibling),
-            )
-        )
-    c_ext = go_ext(
-        C_EXT, coef_send.at[pl.ds(6 + 3 * core, 3)], coef_halo.at[2 * (1 - core), pl.ds(0, 3)]
-    )
-    r_term.wait_recv()
+    for c in r_term:
+        c.wait_recv()
     send_halo(1, 0)
 
     def react(offset, k, f):
-        value = react_factor(offset, n) * state[0, 0, k, f]
+        value = react_factor(offset + 4, n) * state[0, 0, k, f]
         for d in range(1, n):
-            value = value + react_factor(offset + 2 * d, n) * work_init[d - 1, k, f]
+            value = value + react_factor(offset + 4 + 2 * d, n) * work_init[d - 1, k, f]
         return value
 
     def run_stage(eq, stage):
@@ -303,9 +309,10 @@
             for k in range(3):
                 coef_halo[k, 3] = 1.0 / coef_halo[k, 0]
             for d in range(1, n):
-                slab_copies[d - 1].wait_recv()
                 init_copies[d - 1].wait_recv()
-                work_init[d - 1, part] = others[d - 1, :, mine, :]
+            for d in range(2, n):
+                slab_copies[d - 2].wait_recv()
+                work_init[d - 2, part] = others[d - 1, :, mine, :]
         step = (0.5 * time_step, 0.5 * time_step, time_step)
         for k in range(2):
             c = lambda f: state[eq, stage, k, f]
@@ -335,15 +342,24 @@
     last = []
 
     def send_final(eq):
-        target, place = ((after, qn), (before, an))[eq]
-        last.append(go(FINAL + 2 * eq, final.at[eq, other], place.at[:, mine, :], (target, partner)))
-        last.append(go(FINAL + 2 * eq + 1, final.at[eq, part], place.at[:, mine, :], (target, s)))
-        if eq == 1:
-            last.append(go(FINAL + 4, final.at[1, other], ao.at[:, mine, :], (tm, partner)))
-            ao[:, mine, :] = final[1, part]
-
+        place = (qn, an)[eq]
+        last.append(go(final.at[eq, other], place.at[:, mine, :], (tm, partner)))
+        if eq == 1 and n == 2:
+            to_same = make(final.at[eq, part], ao, (after, s), sems - 1, sems - 1)
+            to_cross = make(final.at[eq, other], ao, (after, partner), sems - 2, sems - 1)
+
+            @pl.when(part == after)
+            def _():
+                to_same.start()
+                to_cross.start()
+
+            last.append(to_same)
+            ends.append((to_same, to_cross))
+        place[:, mine, :] = final[eq, part]
+
+    ends = []
     for stage in range(4):
-        for eq in range(2):
+        for eq in (0, 1) if stage < 3 else (1, 0):
             run_stage(eq, stage)
             if stage < 3:
                 send_halo(eq, stage + 1)
@@ -354,6 +370,12 @@
         c.wait_recv()
     for c in started:
         c.wait_send()
+    for to_same, to_cross in ends:
+
+        @pl.when(part == after)
+        def _():
+            to_same.wait_send()
+            to_cross.wait_send()
 
     @pl.when(has_ext)
     def _():
@@ -366,12 +388,14 @@
     half = ny // 2
     f32 = jnp.float32
     plane = jax.ShapeDtypeStruct((5, ny, nz), f32)
+    chunk = jax.ShapeDtypeStruct((5, ny // n, nz), f32)
     vmem = pl.BlockSpec(memory_space=pltpu.VMEM)
-    sems = SLAB + 2 * (n - 1) + 2
+    sems = 48 + 2 * n
+    hbm = pl.BlockSpec(memory_space=pltpu.HBM)
     return pl.pallas_call(
-        functools.partial(kernel, n, count),
-        out_shape=[jax.ShapeDtypeStruct((n - 1, 5, ny, nz), f32), plane, plane, plane],
-        in_specs=[vmem] * 7,
+        functools.partial(kernel, n, count, sems),
+        out_shape=[jax.ShapeDtypeStruct((n - 1, 5, ny, nz), f32), plane, plane, chunk],
+        in_specs=[hbm] * 7,
         out_specs=[vmem] * 4,
         scratch_shapes=[
             pltpu.VMEM((2, 4, 2, 5, half, nz), f32),
@@ -380,13 +404,15 @@
             pltpu.VMEM((2, 4, 2, 16, nz), f32),
             pltpu.VMEM((2, 7, half, nz), f32),
             pltpu.VMEM((3, 4, half, nz), f32),
-            pltpu.VMEM((12, half, nz), f32),
+            pltpu.VMEM((6, half, nz), f32),
             pltpu.VMEM((2, 2, 5, half, nz), f32),
             pltpu.VMEM((2, 5, half, nz), f32),
             pltpu.VMEM((n - 1, 2, 5, half, nz), f32),
             pltpu.VMEM((2, 2, 5, half, nz), f32),
+            pltpu.VMEM(args[2].shape, f32),
             pltpu.SemaphoreType.DMA((sems,)),
             pltpu.SemaphoreType.DMA((sems,)),
+            pltpu.SemaphoreType.DMA((6,)),
         ],
         compiler_params=pltpu.CompilerParams(
             collective_id=0, has_side_effects=True, vmem_limit_bytes=40 * 1024 * 1024
@@ -421,14 +447,13 @@
     force = sum(factors[2 * k + r] * forcing[k, r, :, 0] for k in range(NFREQ) for r in range(2))
     next_initial = qn + (time_step / 6.0) * force
     next_terminal = an + (time_step / 6.0) * react(2)
-    adjoint = ao + (time_step / 6.0) * react(0)
     if n == 2:
         rows = initial.shape[3] // n
-        own = lax.dynamic_slice_in_dim(adjoint, tm * rows, rows, axis=1)
-        far = lax.dynamic_slice_in_dim(next_terminal, tm * rows, rows, axis=1)
-        projection = amplitudes([own, far], [0, 1])[:, :, :, None]
+        chunk = lambda v: lax.dynamic_slice_in_dim(v, tm * rows, rows, axis=1)
+        own = ao + (time_step / 6.0) * chunk(react(0))
+        projection = amplitudes([own, chunk(next_terminal)], [0, 1])[:, :, :, None]
     else:
-        projection = amplitudes([adjoint], [0])[:, :, :, None]
+        projection = amplitudes([next_terminal], [1])[:, :, :, None]
         projection = lax.psum_scatter(projection, "tm", scatter_dimension=4, tiled=True)
     return (next_initial[None, :, None], next_terminal[None, :, None], response, projection)
 

time: 52.8 us -> 53.1 us (level)
  the two profiles are of different devices: /device:TPU:17 before, /device:TPU:13 now
where the time goes in v2:
time: 53.1 us; the launch traced here: 52.8 us
  Pallas kernels  43.5 us (82%)
  local copies, waits for them, and re-layouts  4.66 us (9%)
  other arithmetic  3.91 us (7%)
  between operations  0.71 us (1%)
    pallas_call x1, Pallas kernels, exchange(): pl.pallas_call(functools.partial(kernel, n, count, sems), out_shape=[jax....  43.5 us
    unnamed x16, local copies, waits for them, and re-layouts  4.66 us
    another operation x4, other arithmetic, amplitudes(): return jnp.stack(rows).reshape((NFREQ, 2) + fields[0].shape)  1.92 us

profile of v2, /device:TPU:13, one launch (start us, length us, event | category | flops | bytes accessed | tf_op | source)
XLA Modules:
  0.0 52.8 jit_solution(58745632527915087)
XLA Ops:
  0.7 0.0 copy-start.1
  0.7 0.0 copy-start.2
  0.7 1.0 %fusion.14 = f32[5,96,128]{2,1,0:T(8,128)S(1)} fusion(f32[1,5,1,96,128]{4,3,2,1,0:T(8,128)} %init.1), kind=kLoop, calls=%fused_computation.27 | loop fusion | flops 61440 | bytes 491520 | tf_op jit(solution)/shard_map/mul | solution.py:443
  1.7 0.0 copy-done.1
  1.7 0.1 copy-done.2
  1.8 0.0 copy-start
  1.8 1.2 %copy-done = f32[2,2,5,1,96,128]{5,4,3,2,1,0:T(8,128)S(1)} copy-done((f32[2,2,5,1,96,128]{5,4,3,2,1,0:T(8,128)S(1)}, f32[2,2,5,1,96,128]{5,4,3,2,1,0:T(8,128)}, u32[]{:S(2)}) %copy-start) | copy-done | bytes 983064
  3.0 0.0 copy-start.3
  3.0 0.9 %copy-done.3 = f32[3,1,96,128]{3,2,1,0:T(8,128)S(1)} copy-done((f32[3,1,96,128]{3,2,1,0:T(8,128)S(1)}, f32[3,1,96,128]{3,2,1,0:T(8,128)}, u32[]{:S(2)}) %copy-start.3) | copy-done | bytes 147480
  3.9 0.0 copy-start.4
  3.9 0.8 %copy-done.4 = f32[1,96,128]{2,1,0:T(8,128)S(1)} copy-done((f32[1,96,128]{2,1,0:T(8,128)S(1)}, f32[1,96,128]{2,1,0:T(8,128)}, u32[]{:S(2)}) %copy-start.4) | copy-done | bytes 49176
  4.7 0.0 copy-start.5
  4.7 0.8 %copy-done.5 = f32[1,96,128]{2,1,0:T(8,128)S(1)} copy-done((f32[1,96,128]{2,1,0:T(8,128)S(1)}, f32[1,96,128]{2,1,0:T(8,128)}, u32[]{:S(2)}) %copy-start.5) | copy-done | bytes 49176
  5.5 0.0 copy-start.6
  5.5 0.8 %copy-done.6 = f32[1,96,128]{2,1,0:T(8,128)S(1)} copy-done((f32[1,96,128]{2,1,0:T(8,128)S(1)}, f32[1,96,128]{2,1,0:T(8,128)}, u32[]{:S(2)}) %copy-start.6) | copy-done | bytes 49176
  6.3 43.5 %shard_map.102 = (f32[1,5,96,128]{3,2,1,0:T(8,128)S(1)}, f32[5,96,128]{2,1,0:T(8,128)S(1)}, f32[5,96,128]{2,1,0:T(8,128)S(1)}, f32[5,48,128]{2,1,0:T(8,128)S(1)}) custom-call(f32[1,5,1,96,128]{4,3,2,1,0:T(8,128)S(1)} %copy-done.1, f32[1,5,1,96,128]{4,3,2,1,0:T(8,128)S(1)} %copy-done.2, f32[2,2,5,1,96,128]{5,4,3,2,1,0:T(8,128)S(1)} %copy-done, ...), custom_call_target="tpu_custom_call" | custom-call | tf_op jit(solution)/shard_map/pallas_call | solution.py:395
  49.8 0.8 %fusion.4 = f32[1,5,1,96,128]{4,3,2,1,0:T(8,128)} fusion(f32[5,96,128]{2,1,0:T(8,128)S(1)} %get-tuple-element.8, f32[2,2,5,1,96,128]{5,4,2,3,1,0:T(8,128)S(1)} %bitcast.64, f32[]{:T(128)S(6)} %select_n.36, f32[]{:T(128)S(6)} %select_n.35), kind=kLoop, calls=%fused_computation.7 | loop fusion | flops 491520 | bytes 1474568
  50.7 0.0 copy-start.7
  50.7 0.2 fusion.6
  50.9 1.0 %pad_maximum_fusion = f32[4,5,96,128]{3,2,1,0:T(8,128)} fusion(f32[1,5,96,128]{3,2,1,0:T(8,128)S(1)} %get-tuple-element.21, f32[1,5,96,128]{3,2,1,0:T(8,128)S(1)} %get-tuple-element.20, f32[1,5,96,128]{3,2,1,0:T(8,128)S(1)} %get-tuple-element.19, f32[1,5,96,128]{3,2,1,0:T(8,128)S(1)} %get-tuple-element.18), kind=kLoop, calls=%fused_computation | loop fusion | flops 737280 | bytes 1966080 | tf_op jit(solution)/shard_map/stack | solution.py:440
  51.9 0.0 copy-done.7
  51.9 0.8 %pad_maximum_fusion.1 = f32[4,5,48,128]{3,2,1,0:T(8,128)} fusion(f32[1,5,48,128]{3,2,1,0:T(8,128)S(1)} %get-tuple-element.24, f32[1,5,48,128]{3,2,1,0:T(8,128)S(1)} %get-tuple-element.23, f32[1,5,48,128]{3,2,1,0:T(8,128)S(1)} %get-tuple-element.22, f32[1,5,48,128]{3,2,1,0:T(8,128)S(1)} %get-tuple-element.16), kind=kLoop, calls=%fused_computation.1 | loop fusion | flops 368640 | bytes 983040 | tf_op jit(solution)/shard_map/stack | solution.py:440
  (3 shorter events, 0.1 us)
Async XLA Ops:
  0.7 1.1 %copy-start.1 = (f32[1,5,1,96,128]{4,3,2,1,0:T(8,128)S(1)}, f32[1,5,1,96,128]{4,3,2,1,0:T(8,128)}, u32[]{:S(2)}) copy-start(f32[1,5,1,96,128]{4,3,2,1,0:T(8,128)} %init.1) | copy-start | bytes 737284
  0.7 1.2 %copy-start.2 = (f32[1,5,1,96,128]{4,3,2,1,0:T(8,128)S(1)}, f32[1,5,1,96,128]{4,3,2,1,0:T(8,128)}, u32[]{:S(2)}) copy-start(f32[1,5,1,96,128]{4,3,2,1,0:T(8,128)} %term.1) | copy-start | bytes 737284
  1.8 1.2 %copy-start = (f32[2,2,5,1,96,128]{5,4,3,2,1,0:T(8,128)S(1)}, f32[2,2,5,1,96,128]{5,4,3,2,1,0:T(8,128)}, u32[]{:S(2)}) copy-start(f32[2,2,5,1,96,128]{5,4,3,2,1,0:T(8,128)} %forcing_hbm.1) | copy-start | bytes 2949124
  3.0 0.9 %copy-start.3 = (f32[3,1,96,128]{3,2,1,0:T(8,128)S(1)}, f32[3,1,96,128]{3,2,1,0:T(8,128)}, u32[]{:S(2)}) copy-start(f32[3,1,96,128]{3,2,1,0:T(8,128)} %vel.1) | copy-start | bytes 442372
  3.9 0.8 %copy-start.4 = (f32[1,96,128]{2,1,0:T(8,128)S(1)}, f32[1,96,128]{2,1,0:T(8,128)}, u32[]{:S(2)}) copy-start(f32[1,96,128]{2,1,0:T(8,128)} %dens.1) | copy-start | bytes 147460
  4.7 0.8 %copy-start.5 = (f32[1,96,128]{2,1,0:T(8,128)S(1)}, f32[1,96,128]{2,1,0:T(8,128)}, u32[]{:S(2)}) copy-start(f32[1,96,128]{2,1,0:T(8,128)} %pres.1) | copy-start | bytes 147460
  5.5 0.8 %copy-start.6 = (f32[1,96,128]{2,1,0:T(8,128)S(1)}, f32[1,96,128]{2,1,0:T(8,128)}, u32[]{:S(2)}) copy-start(f32[1,96,128]{2,1,0:T(8,128)} %spon.1) | copy-start | bytes 147460
  50.7 1.2 %copy-start.7 = (f32[5,96,128]{2,1,0:T(8,128)}, f32[5,96,128]{2,1,0:T(8,128)S(1)}, u32[]{:S(2)}) copy-start(f32[5,96,128]{2,1,0:T(8,128)S(1)} %fusion.13) | copy-start | bytes 737284

commit v3 on v2

--- a/solution.py
+++ b/solution.py
@@ -11,6 +11,7 @@
 NFREQ = 2
 viscosity = 0.05
 time_step = 0.25
+ORDER = ((1, 0), (0, 0), (1, 1), (0, 1), (1, 2), (0, 2), (1, 3), (0, 3))
 MESH = pl.DeviceIdType.MESH
 
 def theta(k, half_count, slabs):
@@ -157,6 +158,7 @@
     fetch(pres.at[:, mine, :], coef.at[part, pl.ds(4, 1)])
     fetch(spon.at[:, mine, :], coef.at[part, pl.ds(5, 1)])
     fetch(init.at[0, :, 0, mine, :], work_init.at[n - 2, part])
+    fetch(term.at[0, :, 0, mine, :], state.at[1, 0, part])
 
     pl.semaphore_wait(barrier, len(greet) + has_ext.astype(jnp.int32))
 
@@ -193,6 +195,7 @@
             c.wait_recv()
 
     s_theirs = go(init.at[0, :, 0, theirs, :], others.at[0, :, theirs, :], (after, s))
+    r_term = go(term.at[0, :, 0, theirs, :], state.at[1, 0, part], (tm, partner))
     r_coef = [
         go(dens.at[:, theirs, :], coef.at[part, pl.ds(0, 1)], (tm, partner)),
         go(vel.at[:, 0, theirs, :], coef.at[part, pl.ds(1, 3)], (tm, partner)),
@@ -200,10 +203,6 @@
         go(spon.at[:, theirs, :], coef.at[part, pl.ds(5, 1)], (tm, partner)),
     ]
     s_mine = go(init.at[0, :, 0, mine, :], others.at[0, :, mine, :], (after, s))
-    r_term = [
-        go(term.at[0, :, 0, theirs, :], state.at[1, 0, part], (before, partner)),
-        go(term.at[0, :, 0, mine, :], state.at[1, 0, part], (before, s)),
-    ]
     slab_copies = [
         go(init.at[0, :, 0], others.at[d - 1], (lax.rem(tm + d, n), s)) for d in range(2, n)
     ]
@@ -218,12 +217,11 @@
     fetches[0].wait()
     for f, value in enumerate(force(0, theirs)):
         f_send[0, f] = value
+    s_theirs.wait_recv()
+    r_init = go(others.at[0, :, theirs, :], state.at[0, 0, part], (tm, partner))
     r_f0 = go(f_send.at[0], work_f.at[0, part], (tm, partner))
     for f, value in enumerate(force(1, theirs)):
         f_send[1, f] = value
-    s_theirs.wait_recv()
-    r_init = go(others.at[0, :, theirs, :], state.at[0, 0, part], (tm, partner))
-    r_f1 = go(f_send.at[1], work_f.at[1, part], (tm, partner))
 
     for offset in range(2):
         for f, value in enumerate(force(offset, mine)):
@@ -280,6 +278,8 @@
         for k in range(2)
     ]
     c_ext = go_ext(coef_send.at[pl.ds(3 * core, 3)], coef_halo.at[2 * (1 - core), pl.ds(0, 3)])
+    r_term.wait_recv()
+    send_halo(1, 0)
     s_mine.wait_recv()
     state[0, 0, part] = others[0, :, mine, :]
     r_init.wait_recv()
@@ -288,14 +288,12 @@
         go(state.at[0, 0, other], work_init.at[d - 1, other], (lax.rem(tm + d, n), s))
         for d in range(1, n)
     ]
-    for c in r_term:
-        c.wait_recv()
-    send_halo(1, 0)
+    r_f1 = go(f_send.at[1], work_f.at[1, part], (tm, partner))
 
     def react(offset, k, f):
-        value = react_factor(offset + 4, n) * state[0, 0, k, f]
+        value = react_factor(offset + 2, n) * state[0, 0, k, f]
         for d in range(1, n):
-            value = value + react_factor(offset + 4 + 2 * d, n) * work_init[d - 1, k, f]
+            value = value + react_factor(offset + 2 + 2 * d, n) * work_init[d - 1, k, f]
         return value
 
     def run_stage(eq, stage):
@@ -342,40 +340,43 @@
     last = []
 
     def send_final(eq):
-        place = (qn, an)[eq]
-        last.append(go(final.at[eq, other], place.at[:, mine, :], (tm, partner)))
-        if eq == 1 and n == 2:
-            to_same = make(final.at[eq, part], ao, (after, s), sems - 1, sems - 1)
-            to_cross = make(final.at[eq, other], ao, (after, partner), sems - 2, sems - 1)
-
-            @pl.when(part == after)
+        if eq == 0:
+            last.append(go(final.at[0, other], qn.at[:, mine, :], (tm, partner)))
+            qn[:, mine, :] = final[0, part]
+            return
+        last.append(go(final.at[1, other], an.at[:, mine, :], (before, partner)))
+        last.append(go(final.at[1, part], an.at[:, mine, :], (before, s)))
+        if n == 2:
+            c = make(final.at[1, other], ao, (tm, partner), sems - 1, sems - 1)
+
+            @pl.when(part == tm)
             def _():
-                to_same.start()
-                to_cross.start()
-
-            last.append(to_same)
-            ends.append((to_same, to_cross))
-        place[:, mine, :] = final[eq, part]
+                c.start()
+                ao[...] = final[1, part]
+
+            ends.append(c)
 
     ends = []
-    for stage in range(4):
-        for eq in (0, 1) if stage < 3 else (1, 0):
-            run_stage(eq, stage)
-            if stage < 3:
-                send_halo(eq, stage + 1)
-            else:
-                send_final(eq)
+    for eq, stage in ORDER:
+        run_stage(eq, stage)
+        if stage < 3:
+            send_halo(eq, stage + 1)
+        else:
+            send_final(eq)
 
     for c in last:
         c.wait_recv()
     for c in started:
         c.wait_send()
-    for to_same, to_cross in ends:
-
-        @pl.when(part == after)
+    for c in ends:
+
+        @pl.when(part == tm)
         def _():
-            to_same.wait_send()
-            to_cross.wait_send()
+            c.wait_send()
+
+        @pl.when(part != tm)
+        def _():
+            c.wait_recv()
 
     @pl.when(has_ext)
     def _():
@@ -412,10 +413,10 @@
             pltpu.VMEM(args[2].shape, f32),
             pltpu.SemaphoreType.DMA((sems,)),
             pltpu.SemaphoreType.DMA((sems,)),
-            pltpu.SemaphoreType.DMA((6,)),
+            pltpu.SemaphoreType.DMA((7,)),
         ],
         compiler_params=pltpu.CompilerParams(
-            collective_id=0, has_side_effects=True, vmem_limit_bytes=40 * 1024 * 1024
+            collective_id=0, has_side_effects=True, vmem_limit_bytes=60 * 1024 * 1024
         ),
     )(*args)
 

time: 53.1 us -> 47.2 us (0.89)
  the two profiles are of different devices: /device:TPU:13 before, /device:TPU:17 now
where the time goes in v3:
time: 47.2 us; the launch traced here: 46.3 us
  Pallas kernels  39.8 us (84%)
  other arithmetic  4.85 us (10%)
  local copies, waits for them, and re-layouts  0.85 us (2%)
  between operations  0.75 us (2%)
    pallas_call x1, Pallas kernels, exchange(): pl.pallas_call(functools.partial(kernel, n, count, sems), out_shape=[jax....  39.8 us
    another operation x4, other arithmetic, amplitudes(): return jnp.stack(rows).reshape((NFREQ, 2) + fields[0].shape)  1.9 us
    unnamed x1, other arithmetic  1.78 us
    mul x1, other arithmetic, react(): return sum((react_factor(offset + 2 * d, n) * states[d] for d in range(n)))  0.96 us

profile of v3, /device:TPU:17, one launch (start us, length us, event | category | flops | bytes accessed | tf_op | source)
XLA Modules:
  0.0 46.3 jit_solution(5285073891924562232)
XLA Ops:
  0.7 1.0 %fusion.14 = f32[5,96,128]{2,1,0:T(8,128)S(1)} fusion(f32[1,5,1,96,128]{4,3,2,1,0:T(8,128)} %init.1), kind=kLoop, calls=%fused_computation.27 | loop fusion | flops 61440 | bytes 491520 | tf_op jit(solution)/shard_map/mul | solution.py:444
  1.6 0.0 copy-start
  1.6 39.8 %shard_map.102 = (f32[1,5,96,128]{3,2,1,0:T(8,128)}, f32[5,96,128]{2,1,0:T(8,128)}, f32[5,96,128]{2,1,0:T(8,128)}, f32[5,48,128]{2,1,0:T(8,128)}) custom-call(f32[1,5,1,96,128]{4,3,2,1,0:T(8,128)} %init.1, f32[1,5,1,96,128]{4,3,2,1,0:T(8,128)} %term.1, f32[2,2,5,1,96,128]{5,4,3,2,1,0:T(8,128)} %forcing_hbm.1, f32[1,96,128]{2,1,0:T(8,128)} %dens.1, ...), custom_call_target="tpu_custom_call" | custom-call | tf_op jit(solution)/shard_map/pallas_call | solution.py:396
  41.5 0.0 copy-done
  41.5 0.0 copy-start.1
  41.5 0.0 copy-start.3
  41.5 0.0 copy-start.4
  41.5 1.8 %fusion.4 = f32[1,5,1,96,128]{4,3,2,1,0:T(8,128)} fusion(f32[5,96,128]{2,1,0:T(8,128)} %get-tuple-element.8, f32[2,2,5,1,96,128]{5,4,2,3,1,0:T(8,128)S(1)} %bitcast.64, f32[]{:T(128)S(6)} %select_n.36, f32[]{:T(128)S(6)} %select_n.35), kind=kLoop, calls=%fused_computation.7 | loop fusion | flops 491520 | bytes 1474568
  43.3 0.0 copy-done.1
  43.3 0.0 copy-done.3
  43.3 0.0 copy-done.4
  43.3 0.0 copy-start.2
  43.4 0.0 copy-start.5
  43.4 0.2 fusion.6
  43.5 0.8 %copy-done.5 = f32[5,48,128]{2,1,0:T(8,128)S(1)} copy-done((f32[5,48,128]{2,1,0:T(8,128)S(1)}, f32[5,48,128]{2,1,0:T(8,128)}, u32[]{:S(2)}) %copy-start.5) | copy-done | bytes 122904
  44.4 1.0 %pad_maximum_fusion = f32[4,5,96,128]{3,2,1,0:T(8,128)} fusion(f32[1,5,96,128]{3,2,1,0:T(8,128)S(1)} %get-tuple-element.21, f32[1,5,96,128]{3,2,1,0:T(8,128)S(1)} %get-tuple-element.20, f32[1,5,96,128]{3,2,1,0:T(8,128)S(1)} %get-tuple-element.19, f32[1,5,96,128]{3,2,1,0:T(8,128)S(1)} %get-tuple-element.18), kind=kLoop, calls=%fused_computation | loop fusion | flops 737280 | bytes 1966080 | tf_op jit(solution)/shard_map/stack | solution.py:441
  45.4 0.0 copy-done.2
  45.4 0.8 %pad_maximum_fusion.1 = f32[4,5,48,128]{3,2,1,0:T(8,128)} fusion(f32[1,5,48,128]{3,2,1,0:T(8,128)S(1)} %get-tuple-element.24, f32[1,5,48,128]{3,2,1,0:T(8,128)S(1)} %get-tuple-element.23, f32[1,5,48,128]{3,2,1,0:T(8,128)S(1)} %get-tuple-element.22, f32[1,5,48,128]{3,2,1,0:T(8,128)S(1)} %get-tuple-element.16), kind=kLoop, calls=%fused_computation.1 | loop fusion | flops 368640 | bytes 983040 | tf_op jit(solution)/shard_map/stack | solution.py:441
  (3 shorter events, 0.1 us)
Async XLA Ops:
  1.6 39.8 %copy-start = (f32[2,2,5,1,96,128]{5,4,3,2,1,0:T(8,128)S(1)}, f32[2,2,5,1,96,128]{5,4,3,2,1,0:T(8,128)}, u32[]{:S(2)}) copy-start(f32[2,2,5,1,96,128]{5,4,3,2,1,0:T(8,128)} %forcing_hbm.1) | copy-start | bytes 2949124
  41.5 1.8 %copy-start.1 = (f32[1,5,1,96,128]{4,3,2,1,0:T(8,128)S(1)}, f32[1,5,1,96,128]{4,3,2,1,0:T(8,128)}, u32[]{:S(2)}) copy-start(f32[1,5,1,96,128]{4,3,2,1,0:T(8,128)} %init.1) | copy-start | bytes 737284
  41.5 1.8 %copy-start.3 = (f32[1,5,96,128]{3,2,1,0:T(8,128)S(1)}, f32[1,5,96,128]{3,2,1,0:T(8,128)}, u32[]{:S(2)}) copy-start(f32[1,5,96,128]{3,2,1,0:T(8,128)} %get-tuple-element.10) | copy-start | bytes 737284
  41.5 1.8 %copy-start.4 = (f32[5,96,128]{2,1,0:T(8,128)S(1)}, f32[5,96,128]{2,1,0:T(8,128)}, u32[]{:S(2)}) copy-start(f32[5,96,128]{2,1,0:T(8,128)} %get-tuple-element.9) | copy-start | bytes 737284
  43.3 2.1 %copy-start.2 = (f32[5,96,128]{2,1,0:T(8,128)}, f32[5,96,128]{2,1,0:T(8,128)S(1)}, u32[]{:S(2)}) copy-start(f32[5,96,128]{2,1,0:T(8,128)S(1)} %fusion.13) | copy-start | bytes 737284
  43.4 1.0 %copy-start.5 = (f32[5,48,128]{2,1,0:T(8,128)S(1)}, f32[5,48,128]{2,1,0:T(8,128)}, u32[]{:S(2)}) copy-start(f32[5,48,128]{2,1,0:T(8,128)} %get-tuple-element.11) | copy-start | bytes 368644
